TPU v7x, 32 devices: a whole 2x2x4 slice. The times are simulated.
32 devices in a mesh: seq: 8 (over z, y), head: 4 (over x, core).
Axes of the slice: x: 2, y: 2, z: 4, core: 2. Of those that a mesh axis runs over, the one named last changes fastest.
Arguments:
- queries: bfloat16 [4096, 4096], P('seq', 'head'), may hold values from -4 to 4
- key_vectors: bfloat16 [4096, 4096], P('seq', 'head'), may hold values from -6 to 6
- output_grad: bfloat16 [4096, 4096], P('seq', 'head'), may hold values from -6 to 6
- value_weight: bfloat16 [6144, 4096], P('seq', 'head'), may hold values from -0.078125 to 0.078125
- decay_rate: float32 [32], P('head'), may hold values from 4.8828125e-05 to 0.035
- doc_lengths: int32 [4], replicated, may hold values from 1 to 2048, 4096 in all
- owner_block: int32 [4096, 1], P('seq'), may hold values from 0 to 31; in each aligned block of 128 rows (0 to 127, 128 to 255, ...) at most 8 rows name the same one
- row_offset: int32 [4096], P('seq'), may hold values from 0 to 3127
Outputs:
- row_grads: bfloat16 [32, 32, 8, 6144], P(('seq', 'head'))
Inputs may be any that keep to these rules, and one draw needn't show every extreme that they name: `doc_lengths`: the longest document has exactly 2048 positions. `owner_block`: in each aligned block of 128 positions no owner is named more than 8 times; some block names some owner exactly 8 times.
All inputs are finite; a program needn't handle non-finite values.
Results may differ from a plain program's by a relative error of at most 0.0071.
Values may be sent and summed in bfloat16 or wider, within the bound.
A program may use at most 128 MiB of HBM per device.

v0:
```python
import jax
import jax.numpy as jnp
from jax import lax
from jax.sharding import PartitionSpec as P

VOCAB = 100096


def carried_in(value, axis, combine, identity):
    size, here = (lax.axis_size(axis), lax.axis_index(axis))
    everything = jax.tree.map(lambda part: lax.all_gather(part, axis), value)
    start = jax.tree.map(
        lambda part, zero: jnp.broadcast_to(jnp.asarray(zero, part.dtype), part.shape),
        value,
        identity,
    )

    def hop(k, before):
        at = size - 1 - k
        reached = at > here
        new = combine(before, jax.tree.map(lambda part: part[at], everything))
        return jax.tree.map(lambda a, b: jnp.where(reached, a, b), new, before)

    return lax.fori_loop(0, size, hop, start)


def doc_of(positions, doc_ends):
    return jnp.sum((positions[:, None] >= doc_ends[None, :]).astype(jnp.int32), axis=1)


def intra_terms(query_blk, key_blk, grad_blk, decay_rates, doc_blk, pos_blk):
    head_dim = query_blk.shape[-1]
    scores = (
        jnp.einsum("she,the->hst", key_blk, query_blk, preferred_element_type=jnp.float32)
        / head_dim
    )
    distance = pos_blk[None, :] - pos_blk[:, None]
    allowed = (distance >= 0) & (doc_blk[:, None] == doc_blk[None, :])
    spans = jnp.maximum(distance, 0).astype(jnp.float32)
    decayed = jnp.where(allowed[None], jnp.exp(-decay_rates[:, None, None] * spans[None]), 0.0)
    weights = (decayed * scores).astype(jnp.bfloat16)
    return jnp.einsum("hst,thf->shf", weights, grad_blk, preferred_element_type=jnp.float32)


def state_terms(query_blk, grad_blk, decay_rates, doc_blk, pos_blk, doc_before, pos_before):
    spans = (pos_blk - pos_before).astype(jnp.float32)
    lead_decay = jnp.where(
        (doc_blk == doc_before)[:, None], jnp.exp(-decay_rates[None, :] * spans[:, None]), 0.0
    )
    scaled = (query_blk.astype(jnp.float32) * lead_decay[:, :, None]).astype(jnp.bfloat16)
    local_state = jnp.einsum("the,thf->hef", scaled, grad_blk, preferred_element_type=jnp.float32)
    whole_span = (pos_blk[-1] - pos_before).astype(jnp.float32)
    link_decay = jnp.where(doc_blk[-1] == doc_before, jnp.exp(-decay_rates * whole_span), 0.0)
    return (local_state, link_decay)


def inter_terms(key_blk, carried, decay_rates, doc_blk, pos_blk):
    head_dim = key_blk.shape[-1]
    spans = (pos_blk[-1] - pos_blk).astype(jnp.float32)
    tail_decay = jnp.where(
        (doc_blk == doc_blk[-1])[:, None], jnp.exp(-decay_rates[None, :] * spans[:, None]), 0.0
    )
    product = (
        jnp.einsum(
            "she,hef->shf",
            key_blk,
            carried.astype(jnp.bfloat16),
            preferred_element_type=jnp.float32,
        )
        / head_dim
    )
    return product * tail_decay[:, :, None]


def combine(earlier, following):
    return (following[0] * earlier[0], following[1] + following[0][:, None, None] * earlier[1])


def pack_slots(rows_data, owners, offsets, blocks, capacity, owner_count, vocab_rows):
    row_total = owners.shape[0]
    block_width = row_total // blocks
    grouped = owners.reshape(blocks, block_width)
    same_owner = grouped[:, :, None] == grouped[:, None, :]
    lower_index = jnp.arange(block_width, dtype=jnp.int32)
    earlier = lower_index[None, :] < lower_index[:, None]
    slot_rank = jnp.sum((same_owner & earlier[None]).astype(jnp.int32), axis=2)
    block_ids = jnp.arange(blocks, dtype=jnp.int32)[:, None]
    slot_index = (grouped * blocks + block_ids) * capacity + slot_rank
    slot_total = owner_count * blocks * capacity
    source_row = (
        jnp.full((slot_total,), row_total, jnp.int32)
        .at[slot_index.reshape(-1)]
        .set(jnp.arange(row_total, dtype=jnp.int32))
    )
    padded_rows = jnp.concatenate(
        [rows_data, jnp.zeros((1, rows_data.shape[1]), rows_data.dtype)], 0
    )
    padded_offsets = jnp.concatenate([offsets, jnp.full((1,), vocab_rows, jnp.int32)])
    send_rows = padded_rows[source_row].reshape(owner_count, blocks * capacity, rows_data.shape[1])
    send_offsets = padded_offsets[source_row].reshape(owner_count, blocks * capacity)
    return (send_rows, send_offsets)


def per_device(
    queries,
    key_vectors,
    output_grad,
    value_weight,
    decay_rate,
    doc_lengths,
    owner_block,
    row_offset,
):
    n_seq = lax.axis_size("seq")
    n_head = lax.axis_size("head")
    devices_all = n_seq * n_head
    tok_rows = queries.shape[0]
    head_local = decay_rate.shape[0]
    head_dim = queries.shape[1] // head_local
    seq_rank = lax.axis_index("seq")
    first_row = seq_rank * tok_rows
    positions = first_row + jnp.arange(tok_rows, dtype=jnp.int32)
    doc_ends = jnp.cumsum(doc_lengths)
    doc_index = doc_of(positions, doc_ends)
    pos_before = first_row - 1
    doc_before = doc_of(jnp.maximum(pos_before, 0)[None], doc_ends)[0]
    query_blk = queries.reshape(tok_rows, head_local, head_dim)
    key_blk = key_vectors.reshape(tok_rows, head_local, head_dim)
    grad_blk = output_grad.reshape(tok_rows, head_local, head_dim)
    local_state, link_decay = state_terms(
        query_blk, grad_blk, decay_rate, doc_index, positions, doc_before, pos_before
    )
    intra_part = intra_terms(query_blk, key_blk, grad_blk, decay_rate, doc_index, positions)
    identity = (jnp.ones_like(link_decay), jnp.zeros_like(local_state))
    chained = carried_in((link_decay, local_state), "seq", combine, identity)
    carried = chained[1]
    inter_part = inter_terms(key_blk, carried, decay_rate, doc_index, positions)
    value_grad = (
        (intra_part + inter_part).astype(jnp.bfloat16).reshape(tok_rows, head_local * head_dim)
    )
    partial_dx = lax.dot_general(
        value_grad,
        lax.all_gather(value_weight, "seq", axis=0, tiled=True),
        (((1,), (1,)), ((), ())),
        preferred_element_type=jnp.float32,
    )
    rounded = partial_dx.astype(jnp.bfloat16)
    row_width = rounded.shape[1]
    vocab_rows = VOCAB // devices_all
    block_rows = tok_rows // n_head
    capacity = max(2, 2 * block_rows // devices_all)
    owners = owner_block[:, 0]
    send_rows, send_offsets = pack_slots(
        rounded, owners, row_offset, n_head, capacity, devices_all, vocab_rows
    )
    got_rows, got_offsets = (
        lax.all_to_all(send_rows, ("seq", "head"), split_axis=0, concat_axis=0, tiled=True),
        lax.all_to_all(send_offsets, ("seq", "head"), split_axis=0, concat_axis=0, tiled=True),
    )
    grouped = got_rows.reshape(n_seq, n_head, n_head * capacity, row_width)
    head_total = jnp.sum(grouped.astype(jnp.float32), axis=1).reshape(
        devices_all * capacity, row_width
    )
    flat_rows = lax.optimization_barrier(head_total.astype(jnp.bfloat16)).astype(jnp.float32)
    flat_offsets = got_offsets.reshape(n_seq, n_head, n_head * capacity)[:, 0].reshape(
        devices_all * capacity
    )
    summed = jax.ops.segment_sum(flat_rows, flat_offsets, num_segments=vocab_rows + 1)
    row_grads = (
        summed[flat_offsets].astype(jnp.bfloat16).reshape(1, devices_all, capacity, row_width)
    )
    return row_grads


def solution(mesh):
    return jax.shard_map(
        per_device,
        mesh=mesh,
        in_specs=(
            P("seq", "head"),
            P("seq", "head"),
            P("seq", "head"),
            P("seq", "head"),
            P("head"),
            P(),
            P("seq", None),
            P("seq"),
        ),
        out_specs=P(("seq", "head"), None, None, None),
        check_vma=False,
    )
```

profile of v0, /device:TPU:0, one launch (start us, length us, event | category | flops | bytes accessed | tf_op | source)
XLA Modules:
  0.0 765.7 jit_solution(4773180646000199583)
XLA Ops:
  6.6 0.9 reduce-window.4
  7.5 0.7 slice.13
  8.1 0.6 fusion.26
  8.8 0.1 convert_reduce_fusion.1
  8.9 0.6 slice.12
  10.7 1.2 broadcast_compare_fusion.1
  12.6 0.7 subtract_convert_fusion
  13.3 1.5 copy.34
  14.8 1.2 dynamic-slice
  16.7 0.8 fusion.25
  17.4 0.1 exponential_select_fusion
  17.5 2.5 fusion.8
  20.1 0.0 all-gather.5.cloned.1.call-start
  20.1 0.7 all-gather.5.cloned.1.call-update
  20.9 0.2 convert_reduce_fusion
  21.1 2.4 scatter_custom_fusion
  23.6 4.5 gather_fusion
  28.2 0.7 all_to_all.9
  28.8 7.3 all-to-all-start
  36.2 22.1 %all-reduce.1 = f32[64]{0:T(128)S(1)} all-reduce(f32[64]{0:T(128)S(1)} %get-tuple-element.170), channel_id=3, replica_groups=mesh['seq'=8,'head'=4] {'seq'}, use_global_device_ids=true, to_apply=%add.1 | all-reduce | flops 64 | bytes 512
  58.2 0.1 reshape.358
  58.3 0.3 fusion.15
  58.6 1.2 fusion.7
  59.8 6.3 fusion.1
  66.2 30.7 %all-gather.7.cloned.1.call-done = f32[64,128,128]{2,1,0:T(8,128)} async-done(((f32[8,128,128]{2,1,0:T(8,128)}), f32[64,128,128]{2,1,0:T(8,128)}) %all-gather.7.cloned.1.call-update) | async-done | bytes 4194320 | tf_op jit(solution)/shard_map/all_gather | solution.py:11
  96.9 9.9 %while.16 = (s32[]{:T(128)}, f32[8,128,128]{2,1,0:T(8,128)S(1)}, s32[]{:T(128)}, f32[8,8,128,128]{3,2,1,0:T(8,128)}, f32[8,8]{1,0:T(8,128)S(1)}, /*index=5*/s32[]{:T(128)}, s32[]{:T(128)}, s32[]{:T(128)}, s32[]{:T(128)}) while((s32[]{:T(128)}, f32[8,128,128]{2,1,0:T(8,128)S(1)}, s32[]{:T(128)}, f32[8,8,128,128]{3,2,1,0:T(8,128)}, ...), condition=%wide.region_6.7_spmd.clone, body=%wide.region_5.6_spmd.clone.sunk | while | flops 524296 | bytes 1573135 | solution.py:24
  96.9 1.2 fusion.38
  98.1 1.2 fusion.38
  99.4 1.2 fusion.38
  100.6 1.2 fusion.38
  101.8 1.2 fusion.38
  103.0 1.2 fusion.38
  104.2 1.2 fusion.38
  105.5 1.3 fusion.38
  106.8 2.3 fusion.6
  109.1 164.9 %all-gather.5.cloned.1.call-done = bf16[6144,1024]{1,0:T(8,128)(2,1)} async-done(((bf16[768,1024]{1,0:T(8,128)(2,1)}), bf16[6144,1024]{1,0:T(8,128)(2,1)}) %all-gather.5.cloned.1.call-update) | async-done | bytes 12582928 | tf_op jit(solution)/shard_map/all_gather | solution.py:143
  274.0 21.7 %convolution_convert_fusion = bf16[512,6144]{1,0:T(8,128)(2,1)S(1)} fusion(bf16[512,1024]{0,1:T(8,128)(2,1)S(1)} %bitcast.75, bf16[6144,1024]{1,0:T(8,128)(2,1)} %all-gather.5.cloned.1.call-done), kind=kOutput, calls=%fused_computation.9 | convolution fusion | flops 6445596672 | bytes 19922944 | tf_op jit(solution)/shard_map/dot_general | solution.py:141
  295.7 3.2 concatenate.7
  298.9 25.3 %gather_fusion.1 = bf16[1024,6144]{1,0:T(8,128)(2,1)} fusion(bf16[513,6144]{1,0:T(8,128)(2,1)} %concatenate.7, s32[1024]{0:T(1024)S(1)} %fusion.22), kind=kCustom, calls=%fused_computation.1 | custom fusion | bytes 25169920 | tf_op jit(solution)/shard_map/gather | solution.py:99
  324.3 4.0 all-to-all-start.1
  328.3 0.1 broadcast_in_dim_reshape_squeeze.2
  328.4 0.1 reshape.351
  328.5 278.7 %all-to-all-done.1 = bf16[32,32,6144]{2,1,0:T(8,128)(2,1)} async-done(((bf16[32,32,6144]{2,1,0:T(8,128)(2,1)}), bf16[32,32,6144]{2,1,0:T(8,128)(2,1)}, u32[]{:S(2)}, u32[]{:S(2)}) %all-to-all-start.1) | async-done | bytes 12582944 | tf_op jit(solution)/shard_map/all_to_all | solution.py:157
  607.2 9.7 %bitcast_reduce_fusion = bf16[8,32,6144]{2,1,0:T(8,128)(2,1)} fusion(bf16[32,32,6144]{2,1,0:T(8,128)(2,1)} %all-to-all-done.1), kind=kLoop, calls=%fused_computation.8 | loop fusion | flops 4718592 | bytes 15728640 | tf_op jit(solution)/shard_map/reduce_sum | solution.py:161
  616.9 5.3 convert_element_type.105
  622.2 24.4 %broadcast_in_dim.42 = f32[3129,6144]{1,0:T(8,128)} broadcast(f32[]{:T(128)} %constant.72.clone.1), dimensions={} | broadcast | bytes 76898304 | tf_op jit(solution)/shard_map/broadcast_in_dim | solution.py:168
  646.6 91.0 %scatter_fusion = f32[3129,6144]{1,0:T(8,128)} fusion(f32[3129,6144]{1,0:T(8,128)} %broadcast_in_dim.42, s32[256]{0:T(256)S(1)} %reshape.351, f32[256,6144]{1,0:T(8,128)} %convert_element_type.105), kind=kCustom, calls=%fused_computation.4 | custom fusion | flops 1572864 | bytes 18875392 | tf_op jit(solution)/shard_map/scatter-add | solution.py:168
  737.6 21.2 %gather_fusion.2 = bf16[256,6144]{1,0:T(8,128)(2,1)} fusion(f32[3129,6144]{1,0:T(8,128)} %scatter_fusion, s32[1024]{0:T(1024)S(1)} %pad_clamp_fusion), kind=kCustom, calls=%fused_computation.2 | custom fusion | bytes 6292480 | tf_op jit(solution)/shard_map/gather | solution.py:170
  (31 shorter events, 0.2 us)
Async XLA Ops:
  6.5 53.3 %copy-start = (bf16[512,1024]{1,0:T(8,128)(2,1)S(1)}, bf16[512,1024]{1,0:T(8,128)(2,1)}, u32[]{:S(2)}) copy-start(bf16[512,1024]{1,0:T(8,128)(2,1)} %param.11) | copy-start | bytes 3145732
  6.5 14.3 %copy-start.2 = (s32[512,1]{0,1:T(1,128)S(1)}, s32[512,1]{0,1:T(1,128)}, u32[]{:S(2)}) copy-start(s32[512,1]{0,1:T(1,128)} %param.16) | copy-start | bytes 6148
  6.5 17.0 %copy-start.3 = (s32[512]{0:T(512)S(1)}, s32[512]{0:T(512)}, u32[]{:S(2)}) copy-start(s32[512]{0:T(512)} %param.17) | copy-start | bytes 6148
  6.5 90.4 %all-gather.7.cloned.1.call-start = ((), (), s32[]{:S(2)}) async-start(), calls=%async_computation.3 | async-start | bytes 4718592 | tf_op jit(solution)/shard_map/all_gather | solution.py:11
  20.1 253.9 %all-gather.5.cloned.1.call-start = ((), (), s32[]{:S(2)}) async-start(), calls=%async_computation.2 | async-start | bytes 14155776 | tf_op jit(solution)/shard_map/all_gather | solution.py:143
  28.8 295.4 %all-to-all-start = ((s32[32,1,32]{2,1,0:T(1,128)}), s32[32,1,32]{2,1,0:T(1,128)S(1)}, u32[]{:S(2)}, u32[]{:S(2)}) async-start(s32[32,1,32]{2,1,0:T(1,128)} %all_to_all.9), calls=%async_computation | async-start | bytes 32768 | tf_op jit(solution)/shard_map/all_to_all | solution.py:158
  324.3 283.0 %all-to-all-start.1 = ((bf16[32,32,6144]{2,1,0:T(8,128)(2,1)}), bf16[32,32,6144]{2,1,0:T(8,128)(2,1)}, u32[]{:S(2)}, u32[]{:S(2)}) async-start(bf16[32,32,6144]{2,1,0:T(8,128)(2,1)} %bitcast.70), calls=%async_computation.1 | async-start | bytes 25165824 | tf_op jit(solution)/shard_map/all_to_all | solution.py:157
  737.6 21.3 %copy-start.1 = (bf16[512,1024]{1,0:T(8,128)(2,1)S(1)}, bf16[512,1024]{1,0:T(8,128)(2,1)}, u32[]{:S(2)}) copy-start(bf16[512,1024]{1,0:T(8,128)(2,1)} %param.11) | copy-start | bytes 3145732
Sparse Core Ops, SparseCore 0:
  20.2 76.6 all-gather.6
  99.1 174.8 all-gather.4
where the time goes:
time: 765 us; the launch traced here: 766 us
  waiting for transfers between devices  475 us (62%)
  other arithmetic  122 us (16%)
  local copies, waits for them, and re-layouts  86.2 us (11%)
  matrix products  32.9 us (4%)
  blocking collectives  22.1 us (3%)
  between operations  16.2 us (2%)
  starting transfers between devices  11.4 us (1%)
    all_to_all x1, waiting for transfers between devices, per_device(): lax.all_to_all(send_rows, ('seq', 'head'), split_axis=0, concat_axis=0, t...  279 us
    all_gather x1, waiting for transfers between devices, per_device(): lax.all_gather(value_weight, 'seq', axis=0, tiled=True)  165 us
    scatter-add x1, other arithmetic, per_device(): jax.ops.segment_sum(flat_rows, flat_offsets, num_segments=vocab_rows + 1)  91 us
    all_gather x1, waiting for transfers between devices, carried_in(): everything = jax.tree.map(lambda part: lax.all_gather(part, axis), value)  30.7 us
    gather x1, local copies, waits for them, and re-layouts, pack_slots(): padded_rows[source_row]  25.3 us
    broadcast_in_dim x1, local copies, waits for them, and re-layouts, per_device(): jax.ops.segment_sum(flat_rows, flat_offsets, num_segments=vocab_rows + 1)  24.4 us
    unnamed x1, blocking collectives  22.1 us
    dot_general x1, matrix products, per_device(): lax.dot_general(value_grad, lax.all_gather(value_weight, 'seq', axis=0, t...  21.7 us
  transfers between devices with their start and end apart: 4, of which 3 were waited for; matrix products, arithmetic and copies ran while one was open for 10% of the time, Pallas kernels for 0%

commit v1 on v0

v1 whole, which is shorter than its diff:
```python
import jax
import jax.numpy as jnp
from jax import lax
from jax.sharding import PartitionSpec as P

def doc_of(positions, doc_ends):
    return jnp.sum((positions[:, None] >= doc_ends[None, :]).astype(jnp.int32), axis=1)


def intra_terms(query_blk, key_blk, grad_blk, decay_rates, doc_blk, pos_blk):
    head_dim = query_blk.shape[-1]
    scores = (
        jnp.einsum("she,the->hst", key_blk, query_blk, preferred_element_type=jnp.float32)
        / head_dim
    )
    distance = pos_blk[None, :] - pos_blk[:, None]
    allowed = (distance >= 0) & (doc_blk[:, None] == doc_blk[None, :])
    spans = jnp.maximum(distance, 0).astype(jnp.float32)
    decayed = jnp.where(allowed[None], jnp.exp(-decay_rates[:, None, None] * spans[None]), 0.0)
    weights = (decayed * scores).astype(jnp.bfloat16)
    return jnp.einsum("hst,thf->shf", weights, grad_blk, preferred_element_type=jnp.float32)


def state_terms(query_blk, grad_blk, decay_rates, doc_blk, pos_blk, doc_before, pos_before):
    spans = (pos_blk - pos_before).astype(jnp.float32)
    lead_decay = jnp.where(
        (doc_blk == doc_before)[:, None], jnp.exp(-decay_rates[None, :] * spans[:, None]), 0.0
    )
    scaled = (query_blk.astype(jnp.float32) * lead_decay[:, :, None]).astype(jnp.bfloat16)
    local_state = jnp.einsum("the,thf->hef", scaled, grad_blk, preferred_element_type=jnp.float32)
    whole_span = (pos_blk[-1] - pos_before).astype(jnp.float32)
    link_decay = jnp.where(doc_blk[-1] == doc_before, jnp.exp(-decay_rates * whole_span), 0.0)
    return (local_state, link_decay)


def inter_terms(key_blk, carried, decay_rates, doc_blk, pos_blk):
    head_dim = key_blk.shape[-1]
    spans = (pos_blk[-1] - pos_blk).astype(jnp.float32)
    tail_decay = jnp.where(
        (doc_blk == doc_blk[-1])[:, None], jnp.exp(-decay_rates[None, :] * spans[:, None]), 0.0
    )
    product = (
        jnp.einsum(
            "she,hef->shf",
            key_blk,
            carried.astype(jnp.bfloat16),
            preferred_element_type=jnp.float32,
        )
        / head_dim
    )
    return product * tail_decay[:, :, None]


def later_states(local_state, decay_rates, doc_ends, n_seq, tok_rows):
    heads, head_dim, width = local_state.shape
    piece = heads * head_dim // n_seq
    sent = local_state.reshape(n_seq, piece, width)
    got = lax.all_to_all(sent, "seq", split_axis=0, concat_axis=0, tiled=True)
    first = jnp.arange(n_seq, dtype=jnp.int32) * tok_rows
    doc_before = doc_of(jnp.maximum(first - 1, 0), doc_ends)
    doc_last = doc_of(first + tok_rows - 1, doc_ends)
    link = jnp.where(
        (doc_before == doc_last)[:, None], jnp.exp(-decay_rates * float(tok_rows))[None, :], 0.0
    )
    link_rows = jnp.repeat(link, head_dim, axis=1)
    mine = lax.dynamic_slice_in_dim(link_rows, lax.axis_index("seq") * piece, piece, axis=1)
    carried = jnp.zeros((piece, width), jnp.float32)
    states = [carried]
    for block in range(n_seq - 1, 0, -1):
        carried = mine[block][:, None] * carried + got[block]
        states.append(carried)
    back = jnp.stack(states[::-1]).astype(jnp.bfloat16)
    back = lax.all_to_all(back, "seq", split_axis=0, concat_axis=0, tiled=True)
    return back.reshape(heads, head_dim, width)


def slot_matrix(owners, capacity, owner_count):
    width = owners.shape[0]
    lower = jnp.arange(width, dtype=jnp.int32)
    same = (owners[:, None] == owners[None, :]) & (lower[None, :] < lower[:, None])
    slot = owners * capacity + jnp.sum(same.astype(jnp.int32), axis=1)
    slots = jnp.arange(owner_count * capacity, dtype=jnp.int32)
    return (slots[:, None] == slot[None, :]).astype(jnp.bfloat16)


def per_device(
    queries,
    key_vectors,
    output_grad,
    value_weight,
    decay_rate,
    doc_lengths,
    owner_block,
    row_offset,
):
    n_seq = lax.axis_size("seq")
    n_head = lax.axis_size("head")
    devices_all = n_seq * n_head
    n_hi = n_seq // 2
    tok_rows = queries.shape[0]
    head_local = decay_rate.shape[0]
    head_dim = queries.shape[1] // head_local
    seq_rank = lax.axis_index("seq")
    head_rank = lax.axis_index("head")
    block_rows = tok_rows // n_head
    capacity = max(2, 2 * block_rows // devices_all)
    swap = [(i, i ^ 1) for i in range(n_seq)]

    stride = [[2 * i + low for i in range(n_hi)] for low in range(2)]
    weights = lax.all_gather(
        value_weight, "seq", axis=0, tiled=True, axis_index_groups=stride
    )
    half = weights.shape[0]

    tags_own = jnp.stack([owner_block[:, 0], row_offset])
    tags_pair = lax.ppermute(tags_own, "seq", swap)

    first_row = seq_rank * tok_rows
    positions = first_row + jnp.arange(tok_rows, dtype=jnp.int32)
    doc_ends = jnp.cumsum(doc_lengths)
    doc_index = doc_of(positions, doc_ends)
    pos_before = first_row - 1
    doc_before = doc_of(jnp.maximum(pos_before, 0)[None], doc_ends)[0]
    query_blk = queries.reshape(tok_rows, head_local, head_dim)
    key_blk = key_vectors.reshape(tok_rows, head_local, head_dim)
    grad_blk = output_grad.reshape(tok_rows, head_local, head_dim)
    local_state, _ = state_terms(
        query_blk, grad_blk, decay_rate, doc_index, positions, doc_before, pos_before
    )
    carried = later_states(local_state, decay_rate, doc_ends, n_seq, tok_rows)
    intra_part = intra_terms(query_blk, key_blk, grad_blk, decay_rate, doc_index, positions)
    inter_part = inter_terms(key_blk, carried, decay_rate, doc_index, positions)
    value_own = (
        (intra_part + inter_part).astype(jnp.bfloat16).reshape(tok_rows, head_local * head_dim)
    )
    value_pair = lax.ppermute(value_own, "seq", swap)

    def routed(value_rows, tags):
        part = lax.dot_general(
            value_rows, weights, (((1,), (1,)), ((), ())), preferred_element_type=jnp.float32
        ).astype(jnp.bfloat16)
        parts = lax.all_to_all(
            part.reshape(n_head, block_rows, half), "head", split_axis=0, concat_axis=0, tiled=True
        )
        rows = jnp.sum(parts.astype(jnp.float32), axis=0).astype(jnp.bfloat16)
        mine = lax.dynamic_slice_in_dim(tags, head_rank * block_rows, block_rows, axis=1)
        offsets = mine[1]
        marks = jnp.stack([offsets // 64, offsets % 64, jnp.ones_like(offsets)], axis=1)
        marks = jnp.pad(marks.astype(jnp.bfloat16), ((0, 0), (0, 125)))
        places = slot_matrix(mine[0], capacity, devices_all)
        sent = jnp.dot(
            places, jnp.concatenate([rows, marks], axis=1), preferred_element_type=jnp.float32
        ).astype(jnp.bfloat16)
        got = lax.all_to_all(
            sent.reshape(devices_all, capacity, half + 128),
            ("seq", "head"),
            split_axis=0,
            concat_axis=0,
            tiled=True,
        )
        return got.reshape(n_hi, 2, n_head * capacity, half + 128)

    got_own = routed(value_own, tags_own)
    got_pair = routed(value_pair, tags_pair)

    def marks_of(got, low):
        return got[:, low, :, half:half + 3].astype(jnp.float32).reshape(-1, 3)

    seen = [marks_of(got_own, 0), marks_of(got_pair, 0)]
    keys = [jnp.where(m[:, 2] > 0, m[:, 0] * 64.0 + m[:, 1], -1.0) for m in seen]
    whole = jnp.stack([k.reshape(n_hi, -1) for k in keys], axis=1).reshape(-1)
    halves = []
    for low in range(2):
        total = 0.0
        for got, key in ((got_own, keys[low]), (got_pair, keys[1 - low])):
            equal = ((whole[:, None] == key[None, :]) & (whole >= 0)[:, None]).astype(jnp.bfloat16)
            data = got[:, low, :, :half].reshape(-1, half)
            total = total + jnp.dot(equal, data, preferred_element_type=jnp.float32)
        halves.append(total.astype(jnp.bfloat16).reshape(-1, n_hi, half // n_hi))
    row_grads = jnp.stack(halves, axis=2)
    return row_grads.reshape(1, devices_all, capacity, 2 * half)


def solution(mesh):
    return jax.shard_map(
        per_device,
        mesh=mesh,
        in_specs=(
            P("seq", "head"),
            P("seq", "head"),
            P("seq", "head"),
            P("seq", "head"),
            P("head"),
            P(),
            P("seq", None),
            P("seq"),
        ),
        out_specs=P(("seq", "head"), None, None, None),
        check_vma=False,
    )
```

time: 765 us -> 365 us (0.48)
  waiting for transfers between devices: 475 us -> 235 us
  other arithmetic: 122 us -> 21.7 us
  local copies, waits for them, and re-layouts: 86.2 us -> 31.1 us
  blocking collectives: 22.1 us -> 0 us
  starting transfers between devices: 11.4 us -> 29.9 us
    all_to_all x2 -> x6, waiting for transfers between devices: 279 us -> 144 us  [the longest x2 72.5 us: routed(): lax.all_to_all(sent.reshape(devices_all, capacity, half + 128), ('seq', '...]
    all_gather x2 -> x1, waiting for transfers between devices: 196 us -> 63.7 us  [per_device(): lax.all_gather(value_weight, 'seq', axis=0, tiled=True, axis_index_groups...]
    scatter-add x1 -> x0, other arithmetic: 91 us -> none  [per_device(): jax.ops.segment_sum(flat_rows, flat_offsets, num_segments=vocab_rows + 1)]
    gather x3 -> x0, local copies, waits for them, and re-layouts: 51.1 us -> none  [the longest x1 25.3 us: pack_slots(): padded_rows[source_row]]
    ppermute x0 -> x2, waiting for transfers between devices: none -> 25.8 us  [the longest x1 24 us: per_device(): value_pair = lax.ppermute(value_own, 'seq', swap)]
    broadcast_in_dim x1 -> x0, local copies, waits for them, and re-layouts: 24.4 us -> none  [per_device(): jax.ops.segment_sum(flat_rows, flat_offsets, num_segments=vocab_rows + 1)]
    unnamed x1 -> x0, blocking collectives: 22.1 us -> none
    all_to_all x2 -> x6, starting transfers between devices: 11.3 us -> 26.9 us  [the longest x2 9.74 us: routed(): lax.all_to_all(part.reshape(n_head, block_rows, half), 'head', split_axis...]
  transfers between devices with their start and end apart: 4 -> 9, of which waited for: 3 -> 9; matrix products, arithmetic and copies ran while one was open for 10% -> 11% of each run, Pallas kernels for 0% -> 0%
where the time goes in v1:
time: 365 us; the launch traced here: 363 us
  waiting for transfers between devices  235 us (64%)
  matrix products  32.5 us (9%)
  local copies, waits for them, and re-layouts  31.1 us (9%)
  starting transfers between devices  29.9 us (8%)
  other arithmetic  21.7 us (6%)
  between operations  13.7 us (4%)
    all_to_all x2, waiting for transfers between devices, routed(): lax.all_to_all(sent.reshape(devices_all, capacity, half + 128), ('seq', '...  72.5 us
    all_gather x1, waiting for transfers between devices, per_device(): lax.all_gather(value_weight, 'seq', axis=0, tiled=True, axis_index_groups...  63.7 us
    all_to_all x2, waiting for transfers between devices, routed(): lax.all_to_all(part.reshape(n_head, block_rows, half), 'head', split_axis...  32.3 us
    all_to_all x1, waiting for transfers between devices, later_states(): got = lax.all_to_all(sent, 'seq', split_axis=0, concat_axis=0, tiled=True)  29.8 us
    ppermute x1, waiting for transfers between devices, per_device(): value_pair = lax.ppermute(value_own, 'seq', swap)  24 us
    dot_general x2, matrix products, routed(): lax.dot_general(value_rows, weights, (((1,), (1,)), ((), ())), preferred_...  16 us
    another operation x3, local copies, waits for them, and re-layouts, per_device(): row_grads = jnp.stack(halves, axis=2)  14 us
    all_to_all x1, waiting for transfers between devices, later_states(): back = lax.all_to_all(back, 'seq', split_axis=0, concat_axis=0, tiled=True)  9.84 us
  transfers between devices with their start and end apart: 9, of which 9 were waited for; matrix products, arithmetic and copies ran while one was open for 11% of the time, Pallas kernels for 0%

profile of v1, /device:TPU:0, one launch (start us, length us, event | category | flops | bytes accessed | tf_op | source)
XLA Modules:
  0.0 363.4 jit_solution(16118116191913421036)
XLA Ops:
  6.5 0.7 all-gather.2.cloned.1.call-update
  7.9 0.8 reduce-window.4
  9.4 1.5 copy.48
  10.9 0.8 fusion.61
  12.4 1.3 broadcast_compare_fusion
  13.8 1.3 fusion.13
  15.1 7.3 %all-to-all-start = ((f32[8,128,128]{2,1,0:T(8,128)}), f32[8,128,128]{2,1,0:T(8,128)S(1)}, u32[]{:S(2)}, u32[]{:S(2)}) async-start(f32[8,128,128]{2,1,0:T(8,128)} %fusion.13), calls=%async_computation | async-start | bytes 1048576 | tf_op jit(solution)/shard_map/all_to_all | solution.py:58
  22.6 1.0 fusion.20
  23.7 1.2 fusion.12
  24.8 29.8 %all-to-all-done = f32[8,128,128]{2,1,0:T(8,128)S(1)} async-done(((f32[8,128,128]{2,1,0:T(8,128)}), f32[8,128,128]{2,1,0:T(8,128)S(1)}, u32[]{:S(2)}, u32[]{:S(2)}) %all-to-all-start) | async-done | bytes 524320 | tf_op jit(solution)/shard_map/all_to_all | solution.py:58
  54.6 0.8 fusion.59
  56.0 0.7 convert_dynamic-update-slice_fusion.3
  57.3 0.7 convert_dynamic-update-slice_fusion.1
  58.6 0.7 fusion.58
  59.9 3.4 all-to-all-start.1
  63.3 5.4 %fusion.2 = f32[8,512,128]{1,2,0:T(8,128)S(1)} fusion(f32[512,512]{1,0:T(8,128)} %fusion.12, f32[8]{0:T(128)S(1)} %get-tuple-element.37, pred[512,512]{1,0:T(8,128)(4,1)} %fusion.20, bf16[512,8,128]{0,2,1:T(8,128)(2,1)} %bitcast.144, bf16[512,1024]{1,0:T(8,128)(2,1)} %param.10, bf16[512,1024]{1,0:T(8,128)(2,1)S(1)} %copy-done), kind=kOutput, calls=%fused_computation.7 | convolution fusion | flops 1084227584 | bytes 6553632 | tf_op jit(solution)/shard_map/hst,thf->shf/dot_general | solution.py:21
  68.7 9.8 %all-to-all-done.1 = bf16[8,128,128]{2,1,0:T(8,128)(2,1)S(1)} async-done(((bf16[8,128,128]{2,1,0:T(8,128)(2,1)}), bf16[8,128,128]{2,1,0:T(8,128)(2,1)S(1)}, u32[]{:S(2)}, u32[]{:S(2)}) %all-to-all-start.1) | async-done | bytes 262176 | tf_op jit(solution)/shard_map/all_to_all | solution.py:73
  78.6 1.5 fusion.9
  80.0 63.7 %all-gather.2.cloned.1.call-done = bf16[3072,1024]{1,0:T(8,128)(2,1)} async-done(((bf16[768,1024]{1,0:T(8,128)(2,1)}), bf16[3072,1024]{1,0:T(8,128)(2,1)}) %all-gather.2.cloned.1.call-update) | async-done | bytes 6291472 | tf_op jit(solution)/shard_map/all_gather | solution.py:110
  143.7 8.3 %convolution_convert_fusion.3 = bf16[512,3072]{1,0:T(8,128)(2,1)} fusion(bf16[512,1024]{0,1:T(8,128)(2,1)} %bitcast.141, bf16[3072,1024]{1,0:T(8,128)(2,1)} %all-gather.2.cloned.1.call-done), kind=kOutput, calls=%fused_computation.6 | convolution fusion | flops 3222798336 | bytes 10485760 | tf_op jit(solution)/shard_map/dot_general | solution.py:139
  152.0 4.8 %all-to-all-start.2 = ((bf16[4,128,3072]{2,1,0:T(8,128)(2,1)}), bf16[4,128,3072]{2,1,0:T(8,128)(2,1)}, u32[]{:S(2)}, u32[]{:S(2)}) async-start(bf16[4,128,3072]{2,1,0:T(8,128)(2,1)} %bitcast.136), calls=%async_computation.2 | async-start | bytes 6291456 | tf_op jit(solution)/shard_map/all_to_all | solution.py:142
  156.8 1.5 collective-permute-start.1
  158.3 24.0 %collective-permute-done.1 = bf16[512,1024]{0,1:T(8,128)(2,1)S(1)} collective-permute-done((bf16[512,1024]{0,1:T(8,128)(2,1)S(1)}, bf16[512,1024]{0,1:T(8,128)(2,1)S(1)}, u32[]{:S(2)}, u32[]{:S(2)}) %collective-permute-start.1) | collective-permute-done | bytes 1048608 | tf_op jit(solution)/shard_map/ppermute | solution.py:136
  182.3 7.8 %convolution_convert_fusion.2 = bf16[512,3072]{1,0:T(8,128)(2,1)} fusion(bf16[512,1024]{0,1:T(8,128)(2,1)S(1)} %collective-permute-done.1, bf16[3072,1024]{1,0:T(8,128)(2,1)} %all-gather.2.cloned.1.call-done), kind=kOutput, calls=%fused_computation.5 | convolution fusion | flops 3222798336 | bytes 10485760 | tf_op jit(solution)/shard_map/dot_general | solution.py:139
  190.1 3.7 %all-to-all-done.2 = bf16[4,128,3072]{2,1,0:T(8,128)(2,1)} async-done(((bf16[4,128,3072]{2,1,0:T(8,128)(2,1)}), bf16[4,128,3072]{2,1,0:T(8,128)(2,1)}, u32[]{:S(2)}, u32[]{:S(2)}) %all-to-all-start.2) | async-done | bytes 3145760 | tf_op jit(solution)/shard_map/all_to_all | solution.py:142
  193.8 5.0 %all-to-all-start.4 = ((bf16[4,128,3072]{2,1,0:T(8,128)(2,1)}), bf16[4,128,3072]{2,1,0:T(8,128)(2,1)}, u32[]{:S(2)}, u32[]{:S(2)}) async-start(bf16[4,128,3072]{2,1,0:T(8,128)(2,1)} %bitcast.135), calls=%async_computation.4 | async-start | bytes 6291456 | tf_op jit(solution)/shard_map/all_to_all | solution.py:142
  198.8 1.5 collective-permute-start
  200.6 1.8 collective-permute-done
  202.7 2.5 reduce_sum.88
  205.2 1.7 fusion
  206.9 28.6 %all-to-all-done.4 = bf16[4,128,3072]{2,1,0:T(8,128)(2,1)} async-done(((bf16[4,128,3072]{2,1,0:T(8,128)(2,1)}), bf16[4,128,3072]{2,1,0:T(8,128)(2,1)}, u32[]{:S(2)}, u32[]{:S(2)}) %all-to-all-start.4) | async-done | bytes 3145760 | tf_op jit(solution)/shard_map/all_to_all | solution.py:142
  235.5 2.7 all-to-all-start.3
  238.6 2.5 reduce_sum.91
  241.1 1.7 fusion.1
  242.8 34.6 %all-to-all-done.3 = bf16[32,8,3200]{2,1,0:T(8,128)(2,1)S(1)} async-done(((bf16[32,8,3200]{2,1,0:T(8,128)(2,1)}), bf16[32,8,3200]{2,1,0:T(8,128)(2,1)S(1)}, u32[]{:S(2)}, u32[]{:S(2)}) %all-to-all-start.3) | async-done | bytes 1638432 | tf_op jit(solution)/shard_map/all_to_all | solution.py:154
  277.4 3.8 %all-to-all-start.5 = ((bf16[32,8,3200]{2,1,0:T(8,128)(2,1)}), bf16[32,8,3200]{2,1,0:T(8,128)(2,1)}, u32[]{:S(2)}, u32[]{:S(2)}) async-start(bf16[32,8,3200]{2,1,0:T(8,128)(2,1)} %fusion.1), calls=%async_computation.5 | async-start | bytes 3276800 | tf_op jit(solution)/shard_map/all_to_all | solution.py:154
  281.2 1.1 fusion.80
  282.3 37.9 %all-to-all-done.5 = bf16[32,8,3200]{2,1,0:T(8,128)(2,1)} async-done(((bf16[32,8,3200]{2,1,0:T(8,128)(2,1)}), bf16[32,8,3200]{2,1,0:T(8,128)(2,1)}, u32[]{:S(2)}, u32[]{:S(2)}) %all-to-all-start.5) | async-done | bytes 1638432 | tf_op jit(solution)/shard_map/all_to_all | solution.py:154
  320.2 0.8 slice_convert_fusion
  321.0 2.4 fusion.79
  324.8 0.7 fusion.77
  326.3 1.8 fusion.4
  328.1 3.3 stack_reshape.8
  332.5 1.8 fusion.5
  334.3 4.3 %stack_reshape.9 = bf16[256,4,1,768]{3,1,0,2:T(4,128)(2,1)} reshape(bf16[256,3072]{1,0:T(8,128)(2,1)} %fusion.5) | data formatting | bytes 3145728 | tf_op jit(solution)/shard_map/stack;reshape | solution.py:180
  338.5 3.8 %pad_maximum_fusion = bf16[256,4,2,768]{3,1,0,2:T(4,128)(2,1)S(1)} fusion(bf16[256,4,1,768]{3,1,0,2:T(4,128)(2,1)} %stack_reshape.9, bf16[256,4,1,768]{3,1,0,2:T(4,128)(2,1)S(1)} %stack_reshape.8), kind=kLoop, calls=%fused_computation.14 | loop fusion | flops 1572864 | bytes 6291456 | tf_op jit(solution)/shard_map/stack | solution.py:180
  342.3 6.5 %copy.42 = bf16[256,4,2,768]{3,2,1,0:T(2,128)(2,1)} copy(bf16[256,4,2,768]{3,1,0,2:T(4,128)(2,1)S(1)} %pad_maximum_fusion) | data formatting | bytes 6291456 | tf_op jit(solution)/shard_map/stack | solution.py:180
  348.8 7.8 %reshape.796 = bf16[1,32,8,6144]{3,2,1,0:T(8,128)(2,1)} reshape(bf16[256,4,2,768]{3,2,1,0:T(2,128)(2,1)} %copy.42) | data formatting | bytes 6291456 | tf_op jit(solution)/shard_map/reshape | solution.py:181
  (66 shorter events, 9.1 us)
Async XLA Ops:
  6.5 56.8 %copy-start = (bf16[512,1024]{1,0:T(8,128)(2,1)S(1)}, bf16[512,1024]{1,0:T(8,128)(2,1)}, u32[]{:S(2)}) copy-start(bf16[512,1024]{1,0:T(8,128)(2,1)} %param.9) | copy-start | bytes 3145732
  6.5 5.9 %copy-start.8 = (f32[8]{0:T(128)S(1)}, f32[8]{0:T(128)}, u32[]{:S(2)}) copy-start(f32[8]{0:T(128)} %param.12) | copy-start | bytes 100
  6.5 7.3 %copy-start.7 = (bf16[512,1024]{1,0:T(8,128)(2,1)S(1)}, bf16[512,1024]{1,0:T(8,128)(2,1)}, u32[]{:S(2)}) copy-start(bf16[512,1024]{1,0:T(8,128)(2,1)} %param.10) | copy-start | bytes 3145732
  6.5 137.2 %all-gather.2.cloned.1.call-start = ((), (), s32[]{:S(2)}) async-start(), calls=%async_computation.6 | async-start | bytes 7864320 | tf_op jit(solution)/shard_map/all_gather | solution.py:110
  10.9 4.2 %copy-start.4 = (bf16[512,1024]{0,1:T(8,128)(2,1)}, bf16[512,1024]{0,1:T(8,128)(2,1)S(1)}, u32[]{:S(2)}) copy-start(bf16[512,1024]{0,1:T(8,128)(2,1)S(1)} %copy.48) | copy-start | bytes 3145732
  15.1 39.5 %all-to-all-start = ((f32[8,128,128]{2,1,0:T(8,128)}), f32[8,128,128]{2,1,0:T(8,128)S(1)}, u32[]{:S(2)}, u32[]{:S(2)}) async-start(f32[8,128,128]{2,1,0:T(8,128)} %fusion.13), calls=%async_computation | async-start | bytes 1048576 | tf_op jit(solution)/shard_map/all_to_all | solution.py:58
  59.9 18.7 %all-to-all-start.1 = ((bf16[8,128,128]{2,1,0:T(8,128)(2,1)}), bf16[8,128,128]{2,1,0:T(8,128)(2,1)S(1)}, u32[]{:S(2)}, u32[]{:S(2)}) async-start(bf16[8,128,128]{2,1,0:T(8,128)(2,1)} %constant_dynamic-update-slice_fusion), calls=%async_computation.1 | async-start | bytes 524288 | tf_op jit(solution)/shard_map/all_to_all | solution.py:73
  152.0 4.8 %copy-start.3 = (bf16[512,8,128]{0,2,1:T(8,128)(2,1)S(1)}, bf16[512,8,128]{0,2,1:T(8,128)(2,1)}, u32[]{:S(2)}) copy-start(bf16[512,8,128]{0,2,1:T(8,128)(2,1)} %fusion.9) | copy-start | bytes 3145732
  152.0 41.8 %all-to-all-start.2 = ((bf16[4,128,3072]{2,1,0:T(8,128)(2,1)}), bf16[4,128,3072]{2,1,0:T(8,128)(2,1)}, u32[]{:S(2)}, u32[]{:S(2)}) async-start(bf16[4,128,3072]{2,1,0:T(8,128)(2,1)} %bitcast.136), calls=%async_computation.2 | async-start | bytes 6291456 | tf_op jit(solution)/shard_map/all_to_all | solution.py:142
  156.8 25.5 %collective-permute-start.1 = (bf16[512,1024]{0,1:T(8,128)(2,1)S(1)}, bf16[512,1024]{0,1:T(8,128)(2,1)S(1)}, u32[]{:S(2)}, u32[]{:S(2)}) collective-permute-start(bf16[512,1024]{0,1:T(8,128)(2,1)S(1)} %bitcast.142), channel_id=1, source_target_pairs={{0,4},{4,0},{8,12},{12,8},{16,20},{20,16},{24,28},{28,24},{1,5},{5... | collective-permute-start | bytes 3145736 | tf_op jit(solution)/shard_map/ppermute | solution.py:136
  193.8 5.0 %copy-start.5 = (s32[512,1]{0,1:T(1,128)S(1)}, s32[512,1]{0,1:T(1,128)}, u32[]{:S(2)}) copy-start(s32[512,1]{0,1:T(1,128)} %param.14) | copy-start | bytes 6148
  193.8 5.0 %copy-start.6 = (s32[512]{0:T(512)S(1)}, s32[512]{0:T(512)}, u32[]{:S(2)}) copy-start(s32[512]{0:T(512)} %param.15) | copy-start | bytes 6148
  193.8 41.8 %all-to-all-start.4 = ((bf16[4,128,3072]{2,1,0:T(8,128)(2,1)}), bf16[4,128,3072]{2,1,0:T(8,128)(2,1)}, u32[]{:S(2)}, u32[]{:S(2)}) async-start(bf16[4,128,3072]{2,1,0:T(8,128)(2,1)} %bitcast.135), calls=%async_computation.4 | async-start | bytes 6291456 | tf_op jit(solution)/shard_map/all_to_all | solution.py:142
  198.8 3.7 %collective-permute-start = (s32[2,512]{1,0:T(2,128)S(1)}, s32[2,512]{1,0:T(2,128)S(1)}, u32[]{:S(2)}, u32[]{:S(2)}) collective-permute-start(s32[2,512]{1,0:T(2,128)S(1)} %pad_add_fusion), channel_id=1, source_target_pairs={{0,4},{4,0},{8,12},{12,8},{16,20},{20,16},{24,28},{28,24},{1,5},{5... | collective-permute-start | bytes 12296 | tf_op jit(solution)/shard_map/ppermute | solution.py:116
  235.5 41.9 %all-to-all-start.3 = ((bf16[32,8,3200]{2,1,0:T(8,128)(2,1)}), bf16[32,8,3200]{2,1,0:T(8,128)(2,1)S(1)}, u32[]{:S(2)}, u32[]{:S(2)}) async-start(bf16[32,8,3200]{2,1,0:T(8,128)(2,1)} %fusion), calls=%async_computation.3 | async-start | bytes 3276800 | tf_op jit(solution)/shard_map/all_to_all | solution.py:154
  277.4 42.8 %all-to-all-start.5 = ((bf16[32,8,3200]{2,1,0:T(8,128)(2,1)}), bf16[32,8,3200]{2,1,0:T(8,128)(2,1)}, u32[]{:S(2)}, u32[]{:S(2)}) async-start(bf16[32,8,3200]{2,1,0:T(8,128)(2,1)} %fusion.1), calls=%async_computation.5 | async-start | bytes 3276800 | tf_op jit(solution)/shard_map/all_to_all | solution.py:154
  282.3 43.4 %copy-start.2 = (bf16[4,1,32,3072]{3,2,1,0:T(8,128)(2,1)S(1)}, bf16[4,1,32,3072]{3,2,1,0:T(8,128)(2,1)}, u32[]{:S(2)}) copy-start(bf16[4,1,32,3072]{3,2,1,0:T(8,128)(2,1)} %get-tuple-element.21) | copy-start | bytes 2359300
  331.4 1.1 copy-start.1
Sparse Core Ops, SparseCore 0:
  8.9 134.7 all-gather.1

commit v2 on v1

--- a/solution.py
+++ b/solution.py
@@ -1,6 +1,7 @@
 import jax
 import jax.numpy as jnp
 from jax import lax
+from jax.experimental import pallas as pl
 from jax.sharding import PartitionSpec as P
 
 def doc_of(positions, doc_ends):
@@ -81,6 +82,61 @@
     slot = owners * capacity + jnp.sum(same.astype(jnp.int32), axis=1)
     slots = jnp.arange(owner_count * capacity, dtype=jnp.int32)
     return (slots[:, None] == slot[None, :]).astype(jnp.bfloat16)
+
+
+def head_sum(parts):
+    n_head = lax.axis_size("head")
+    head_rank = lax.axis_index("head")
+    step = 1
+    while step < n_head:
+        bit = (head_rank // step) % 2
+        pairs = parts.reshape((parts.shape[0] // 2, 2) + parts.shape[1:])
+        sent = lax.dynamic_index_in_dim(pairs, 1 - bit, axis=1, keepdims=False)
+        kept = lax.dynamic_index_in_dim(pairs, bit, axis=1, keepdims=False)
+        got = lax.ppermute(sent, "head", [(i, i ^ step) for i in range(n_head)])
+        parts = (kept.astype(jnp.float32) + got.astype(jnp.float32)).astype(jnp.bfloat16)
+        step *= 2
+    return parts[0]
+
+
+def merge_kernel(equal_own, equal_pair, rows_own, rows_pair, out):
+    shape = (-1, rows_own.shape[-1])
+    total = jnp.dot(
+        equal_own[0], rows_own[...].reshape(shape), preferred_element_type=jnp.float32
+    )
+    total += jnp.dot(
+        equal_pair[0], rows_pair[...].reshape(shape), preferred_element_type=jnp.float32
+    )
+    out[...] = total.astype(out.dtype)
+
+
+def merged(equal, got_own, got_pair, half):
+    n_hi, _, rows, _ = got_own.shape
+    width = half // n_hi
+    slots = equal.shape[1]
+    if width % 128 == 0 and rows % 16 == 0:
+        matrix = (1, slots, equal.shape[2])
+        data = pl.BlockSpec((n_hi, 1, rows, width), lambda i, low: (0, low, 0, i))
+        return pl.pallas_call(
+            merge_kernel,
+            grid=(n_hi, 2),
+            in_specs=[
+                pl.BlockSpec(matrix, lambda i, low: (low, 0, 0)),
+                pl.BlockSpec(matrix, lambda i, low: (1 - low, 0, 0)),
+                data,
+                data,
+            ],
+            out_specs=pl.BlockSpec((slots, width), lambda i, low: (0, 2 * i + low)),
+            out_shape=jax.ShapeDtypeStruct((slots, 2 * half), jnp.bfloat16),
+        )(equal, equal, got_own, got_pair)
+    halves = []
+    for low in range(2):
+        total = 0.0
+        for got, match in ((got_own, equal[low]), (got_pair, equal[1 - low])):
+            data = got[:, low, :, :half].reshape(-1, half)
+            total = total + jnp.dot(match, data, preferred_element_type=jnp.float32)
+        halves.append(total.astype(jnp.bfloat16).reshape(-1, n_hi, width))
+    return jnp.stack(halves, axis=2).reshape(slots, 2 * half)
 
 
 def per_device(
@@ -134,15 +190,13 @@
         (intra_part + inter_part).astype(jnp.bfloat16).reshape(tok_rows, head_local * head_dim)
     )
     value_pair = lax.ppermute(value_own, "seq", swap)
+    weights, value_pair = lax.optimization_barrier((weights, value_pair))
 
     def routed(value_rows, tags):
         part = lax.dot_general(
             value_rows, weights, (((1,), (1,)), ((), ())), preferred_element_type=jnp.float32
         ).astype(jnp.bfloat16)
-        parts = lax.all_to_all(
-            part.reshape(n_head, block_rows, half), "head", split_axis=0, concat_axis=0, tiled=True
-        )
-        rows = jnp.sum(parts.astype(jnp.float32), axis=0).astype(jnp.bfloat16)
+        rows = head_sum(part.reshape(n_head, block_rows, half))
         mine = lax.dynamic_slice_in_dim(tags, head_rank * block_rows, block_rows, axis=1)
         offsets = mine[1]
         marks = jnp.stack([offsets // 64, offsets % 64, jnp.ones_like(offsets)], axis=1)
@@ -169,15 +223,11 @@
     seen = [marks_of(got_own, 0), marks_of(got_pair, 0)]
     keys = [jnp.where(m[:, 2] > 0, m[:, 0] * 64.0 + m[:, 1], -1.0) for m in seen]
     whole = jnp.stack([k.reshape(n_hi, -1) for k in keys], axis=1).reshape(-1)
-    halves = []
-    for low in range(2):
-        total = 0.0
-        for got, key in ((got_own, keys[low]), (got_pair, keys[1 - low])):
-            equal = ((whole[:, None] == key[None, :]) & (whole >= 0)[:, None]).astype(jnp.bfloat16)
-            data = got[:, low, :, :half].reshape(-1, half)
-            total = total + jnp.dot(equal, data, preferred_element_type=jnp.float32)
-        halves.append(total.astype(jnp.bfloat16).reshape(-1, n_hi, half // n_hi))
-    row_grads = jnp.stack(halves, axis=2)
+    equal = jnp.stack([
+        ((whole[:, None] == key[None, :]) & (whole >= 0)[:, None]).astype(jnp.bfloat16)
+        for key in keys
+    ])
+    row_grads = merged(equal, got_own, got_pair, half)
     return row_grads.reshape(1, devices_all, capacity, 2 * half)
 
 

time: 365 us -> 286 us (0.78)
  waiting for transfers between devices: 235 us -> 185 us
  local copies, waits for them, and re-layouts: 31.1 us -> 12 us
  matrix products: 32.5 us -> 24.5 us
  Pallas kernels: 0 us -> 7.53 us
  starting transfers between devices: 29.9 us -> 24.4 us
    ppermute x0 -> x4, waiting for transfers between devices: none -> 41.8 us  [head_sum(): got = lax.ppermute(sent, 'head', [(i, i ^ step) for i in range(n_head)])]
    all_to_all x2, waiting for transfers between devices: 72.5 us -> 38.7 us  [routed(): lax.all_to_all(sent.reshape(devices_all, capacity, half + 128), ('seq', '...]
    all_to_all x2 -> x0, waiting for transfers between devices: 32.3 us -> none  [routed(): lax.all_to_all(part.reshape(n_head, block_rows, half), 'head', split_axis...]
    all_gather x1, waiting for transfers between devices: 63.7 us -> 46.3 us  [per_device(): lax.all_gather(value_weight, 'seq', axis=0, tiled=True, axis_index_groups...]
    another operation x3 -> x0, local copies, waits for them, and re-layouts: 14 us -> none  [per_device(): row_grads = jnp.stack(halves, axis=2)]
    all_to_all x2 -> x0, starting transfers between devices: 9.74 us -> none  [routed(): lax.all_to_all(part.reshape(n_head, block_rows, half), 'head', split_axis...]
    ppermute x1, waiting for transfers between devices: 24 us -> 15.8 us  [per_device(): value_pair = lax.ppermute(value_own, 'seq', swap)]
    reshape x1 -> x0, local copies, waits for them, and re-layouts: 7.76 us -> none  [per_device(): return row_grads.reshape(1, devices_all, capacity, 2 * half)]
  transfers between devices with their start and end apart: 9 -> 11, of which waited for: 9 -> 8; matrix products, arithmetic and copies ran while one was open for 11% -> 13% of each run, Pallas kernels for 0% -> 0%
where the time goes in v2:
time: 286 us; the launch traced here: 285 us
  waiting for transfers between devices  185 us (65%)
  matrix products  24.5 us (9%)
  starting transfers between devices  24.4 us (9%)
  other arithmetic  18.3 us (6%)
  between operations  13.8 us (5%)
  local copies, waits for them, and re-layouts  12 us (4%)
  Pallas kernels  7.53 us (3%)
    all_gather x1, waiting for transfers between devices, per_device(): lax.all_gather(value_weight, 'seq', axis=0, tiled=True, axis_index_groups...  46.3 us
    ppermute x4, waiting for transfers between devices, head_sum(): got = lax.ppermute(sent, 'head', [(i, i ^ step) for i in range(n_head)])  41.8 us
    all_to_all x2, waiting for transfers between devices, routed(): lax.all_to_all(sent.reshape(devices_all, capacity, half + 128), ('seq', '...  38.7 us
    all_to_all x1, waiting for transfers between devices, later_states(): got = lax.all_to_all(sent, 'seq', split_axis=0, concat_axis=0, tiled=True)  29.8 us
    ppermute x1, waiting for transfers between devices, per_device(): value_pair = lax.ppermute(value_own, 'seq', swap)  15.8 us
    dot_general x2, matrix products, routed(): lax.dot_general(value_rows, weights, (((1,), (1,)), ((), ())), preferred_...  11.5 us
    all_to_all x1, waiting for transfers between devices, later_states(): back = lax.all_to_all(back, 'seq', split_axis=0, concat_axis=0, tiled=True)  9.86 us
    pallas_call x1, Pallas kernels, merged(): pl.pallas_call(merge_kernel, grid=(n_hi, 2), in_specs=[pl.BlockSpec(matri...  7.53 us
  transfers between devices with their start and end apart: 11, of which 8 were waited for; matrix products, arithmetic and copies ran while one was open for 13% of the time, Pallas kernels for 0%

profile of v2, /device:TPU:0, one launch (start us, length us, event | category | flops | bytes accessed | tf_op | source)
XLA Modules:
  0.0 285.3 jit_solution(14772528092759551719)
XLA Ops:
  6.5 0.7 all-gather.2.cloned.1.call-update
  7.9 0.8 reduce-window.4
  9.9 0.7 subtract_convert_fusion
  10.6 0.6 fusion.49
  11.2 1.2 broadcast_compare_fusion
  12.5 2.5 fusion.13
  15.0 7.3 %all-to-all-start = ((f32[8,128,128]{2,1,0:T(8,128)}), f32[8,128,128]{2,1,0:T(8,128)S(1)}, u32[]{:S(2)}, u32[]{:S(2)}) async-start(f32[8,128,128]{2,1,0:T(8,128)} %fusion.13), calls=%async_computation | async-start | bytes 1048576 | tf_op jit(solution)/shard_map/all_to_all | solution.py:59
  22.6 1.0 fusion.20
  23.6 1.2 fusion.12
  24.8 29.8 %all-to-all-done = f32[8,128,128]{2,1,0:T(8,128)S(1)} async-done(((f32[8,128,128]{2,1,0:T(8,128)}), f32[8,128,128]{2,1,0:T(8,128)S(1)}, u32[]{:S(2)}, u32[]{:S(2)}) %all-to-all-start) | async-done | bytes 524320 | tf_op jit(solution)/shard_map/all_to_all | solution.py:59
  54.6 0.8 fusion.47
  56.0 0.7 convert_dynamic-update-slice_fusion.3
  56.7 0.6 convert_dynamic-update-slice_fusion.2
  57.3 0.7 convert_dynamic-update-slice_fusion.1
  58.6 0.7 fusion.46
  59.3 0.6 constant_dynamic-update-slice_fusion
  59.9 3.4 %all-to-all-start.1 = ((bf16[8,128,128]{2,1,0:T(8,128)(2,1)}), bf16[8,128,128]{2,1,0:T(8,128)(2,1)S(1)}, u32[]{:S(2)}, u32[]{:S(2)}) async-start(bf16[8,128,128]{2,1,0:T(8,128)(2,1)} %constant_dynamic-update-slice_fusion), calls=%async_computation.1 | async-start | bytes 524288 | tf_op jit(solution)/shard_map/all_to_all | solution.py:74
  63.3 5.4 %fusion.2 = f32[8,512,128]{1,2,0:T(8,128)S(1)} fusion(f32[512,512]{1,0:T(8,128)} %fusion.12, f32[8]{0:T(128)S(1)} %get-tuple-element.45, pred[512,512]{1,0:T(8,128)(4,1)} %fusion.20, bf16[512,8,128]{0,2,1:T(8,128)(2,1)} %bitcast.149, bf16[512,1024]{1,0:T(8,128)(2,1)} %param.10, bf16[512,1024]{1,0:T(8,128)(2,1)S(1)} %copy-done), kind=kOutput, calls=%fused_computation.7 | convolution fusion | flops 1084227584 | bytes 6553632 | tf_op jit(solution)/shard_map/hst,thf->shf/dot_general | solution.py:22
  68.8 9.9 %all-to-all-done.1 = bf16[8,128,128]{2,1,0:T(8,128)(2,1)S(1)} async-done(((bf16[8,128,128]{2,1,0:T(8,128)(2,1)}), bf16[8,128,128]{2,1,0:T(8,128)(2,1)S(1)}, u32[]{:S(2)}, u32[]{:S(2)}) %all-to-all-start.1) | async-done | bytes 262176 | tf_op jit(solution)/shard_map/all_to_all | solution.py:74
  78.6 1.6 fusion.9
  80.2 1.4 collective-permute-start
  81.6 15.8 %collective-permute-done = bf16[512,1024]{0,1:T(8,128)(2,1)S(1)} collective-permute-done((bf16[512,1024]{0,1:T(8,128)(2,1)}, bf16[512,1024]{0,1:T(8,128)(2,1)S(1)}, u32[]{:S(2)}, u32[]{:S(2)}) %collective-permute-start) | collective-permute-done | bytes 1048608 | tf_op jit(solution)/shard_map/ppermute | solution.py:192
  97.4 46.3 %all-gather.2.cloned.1.call-done = bf16[3072,1024]{1,0:T(8,128)(2,1)} async-done(((bf16[768,1024]{1,0:T(8,128)(2,1)}), bf16[3072,1024]{1,0:T(8,128)(2,1)}) %all-gather.2.cloned.1.call-update) | async-done | bytes 6291472 | tf_op jit(solution)/shard_map/all_gather | solution.py:166
  143.7 6.6 %convolution_convert_fusion.2 = bf16[512,3072]{1,0:T(8,128)(2,1)S(1)} fusion(bf16[512,1024]{0,1:T(8,128)(2,1)S(1)} %collective-permute-done, bf16[3072,1024]{1,0:T(8,128)(2,1)} %all-gather.2.cloned.1.call-done), kind=kOutput, calls=%fused_computation.5 | convolution fusion | flops 3222798336 | bytes 10485760 | tf_op jit(solution)/shard_map/dot_general | solution.py:196
  150.3 1.6 copy-done.3
  152.0 1.3 dynamic-slice_bitcast_fusion
  153.3 1.5 collective-permute-start.3
  155.0 2.0 collective-permute-done.3
  157.2 2.1 fusion.6
  159.5 1.5 collective-permute-start.5
  161.0 4.9 %convolution_convert_fusion.3 = bf16[512,3072]{1,0:T(8,128)(2,1)S(1)} fusion(bf16[512,1024]{0,1:T(8,128)(2,1)} %bitcast.19, bf16[3072,1024]{1,0:T(8,128)(2,1)S(1)} %copy-done.9), kind=kOutput, calls=%fused_computation.6 | convolution fusion | flops 3222798336 | bytes 10485760 | tf_op jit(solution)/shard_map/dot_general | solution.py:196
  166.0 1.4 dynamic-slice_bitcast_fusion.1
  167.5 11.3 %collective-permute-done.5 = bf16[1,128,3072]{2,1,0:T(8,128)(2,1)S(1)} collective-permute-done((bf16[1,128,3072]{2,1,0:T(8,128)(2,1)S(1)}, bf16[1,128,3072]{2,1,0:T(8,128)(2,1)S(1)}, u32[]{:S(2)}, u32[]{:S(2)}) %collective-permute-start.5) | collective-permute-done | bytes 786464 | tf_op jit(solution)/shard_map/ppermute | solution.py:96
  179.0 1.8 fusion.1
  180.7 2.7 all-to-all-start.3
  183.5 2.5 fusion.7
  185.9 1.1 copy-done.2
  187.1 0.9 constant_dynamic-slice_fusion.2
  188.0 1.8 collective-permute-start.2
  190.1 30.5 %collective-permute-done.2 = bf16[1,128,3072]{2,1,0:T(8,128)(2,1)S(1)} collective-permute-done((bf16[1,128,3072]{2,1,0:T(8,128)(2,1)}, bf16[1,128,3072]{2,1,0:T(8,128)(2,1)S(1)}, u32[]{:S(2)}, u32[]{:S(2)}) %collective-permute-start.2) | collective-permute-done | bytes 786464 | tf_op jit(solution)/shard_map/ppermute | solution.py:96
  220.7 1.3 fusion.36
  222.0 1.7 fusion
  223.7 4.7 %all-to-all-start.2 = ((bf16[32,8,3200]{2,1,0:T(8,128)(2,1)}), bf16[32,8,3200]{2,1,0:T(8,128)(2,1)}, u32[]{:S(2)}, u32[]{:S(2)}) async-start(bf16[32,8,3200]{2,1,0:T(8,128)(2,1)} %fusion), calls=%async_computation.2 | async-start | bytes 3276800 | tf_op jit(solution)/shard_map/all_to_all | solution.py:208
  228.8 38.7 %all-to-all-done.2 = bf16[32,8,3200]{2,1,0:T(8,128)(2,1)} async-done(((bf16[32,8,3200]{2,1,0:T(8,128)(2,1)}), bf16[32,8,3200]{2,1,0:T(8,128)(2,1)}, u32[]{:S(2)}, u32[]{:S(2)}) %all-to-all-start.2) | async-done | bytes 1638432 | tf_op jit(solution)/shard_map/all_to_all | solution.py:208
  267.5 0.8 slice.137
  269.1 0.7 fusion.65
  270.2 0.7 add_convert_fusion.2.equal_own.equal_pair
  270.9 7.5 %shard_map.82 = bf16[256,6144]{1,0:T(8,128)(2,1)} custom-call(bf16[2,256,128]{2,1,0:T(8,128)(2,1)} %add_convert_fusion.2.equal_own.equal_pair, bf16[2,256,128]{2,1,0:T(8,128)(2,1)} %add_convert_fusion.2.equal_own.equal_pair, bf16[4,2,32,3200]{3,2,1,0:T(8,128)(2,1)} %bitcast.26.rows_own, bf16[4,2,32,3200]{3,2,1,0:T(8,128)(2,1)} %bitcast.143), custom_call_target="tpu_custom_call" | custom-call | tf_op jit(solution)/shard_map/pallas_call | solution.py:120
  (82 shorter events, 6.2 us)
Async XLA Ops:
  6.5 56.8 %copy-start = (bf16[512,1024]{1,0:T(8,128)(2,1)S(1)}, bf16[512,1024]{1,0:T(8,128)(2,1)}, u32[]{:S(2)}) copy-start(bf16[512,1024]{1,0:T(8,128)(2,1)} %param.9) | copy-start | bytes 3145732
  6.5 2.8 copy-start.5
  6.5 4.7 %copy-start.10 = (f32[8]{0:T(128)S(1)}, f32[8]{0:T(128)}, u32[]{:S(2)}) copy-start(f32[8]{0:T(128)} %param.12) | copy-start | bytes 100
  6.5 137.2 %all-gather.2.cloned.1.call-start = ((), (), s32[]{:S(2)}) async-start(), calls=%async_computation.4 | async-start | bytes 7864320 | tf_op jit(solution)/shard_map/all_gather | solution.py:166
  9.9 12.7 %copy-start.6 = (bf16[512,1024]{0,1:T(8,128)(2,1)}, bf16[512,1024]{0,1:T(8,128)(2,1)S(1)}, u32[]{:S(2)}) copy-start(bf16[512,1024]{0,1:T(8,128)(2,1)S(1)} %copy.61) | copy-start | bytes 3145732
  15.0 39.5 %all-to-all-start = ((f32[8,128,128]{2,1,0:T(8,128)}), f32[8,128,128]{2,1,0:T(8,128)S(1)}, u32[]{:S(2)}, u32[]{:S(2)}) async-start(f32[8,128,128]{2,1,0:T(8,128)} %fusion.13), calls=%async_computation | async-start | bytes 1048576 | tf_op jit(solution)/shard_map/all_to_all | solution.py:59
  59.9 18.7 %all-to-all-start.1 = ((bf16[8,128,128]{2,1,0:T(8,128)(2,1)}), bf16[8,128,128]{2,1,0:T(8,128)(2,1)S(1)}, u32[]{:S(2)}, u32[]{:S(2)}) async-start(bf16[8,128,128]{2,1,0:T(8,128)(2,1)} %constant_dynamic-update-slice_fusion), calls=%async_computation.1 | async-start | bytes 524288 | tf_op jit(solution)/shard_map/all_to_all | solution.py:74
  80.2 17.2 %collective-permute-start = (bf16[512,1024]{0,1:T(8,128)(2,1)}, bf16[512,1024]{0,1:T(8,128)(2,1)S(1)}, u32[]{:S(2)}, u32[]{:S(2)}) collective-permute-start(bf16[512,1024]{0,1:T(8,128)(2,1)} %bitcast.19), channel_id=1, source_target_pairs={{0,4},{4,0},{8,12},{12,8},{16,20},{20,16},{24,28},{28,24},{1,5},{5... | collective-permute-start | bytes 3145736 | tf_op jit(solution)/shard_map/ppermute | solution.py:192
  150.3 1.7 copy-start.3
  150.3 3.0 %copy-start.7 = (s32[512,1]{0,1:T(1,128)S(1)}, s32[512,1]{0,1:T(1,128)}, u32[]{:S(2)}) copy-start(s32[512,1]{0,1:T(1,128)} %param.14) | copy-start | bytes 6148
  150.3 3.0 %copy-start.8 = (s32[512]{0:T(512)S(1)}, s32[512]{0:T(512)}, u32[]{:S(2)}) copy-start(s32[512]{0:T(512)} %param.15) | copy-start | bytes 6148
  153.2 4.0 %collective-permute-start.4 = (bf16[2,128,3072]{2,1,0:T(8,128)(2,1)}, bf16[2,128,3072]{2,1,0:T(8,128)(2,1)S(1)}, u32[]{:S(2)}, u32[]{:S(2)}) collective-permute-start(bf16[2,128,3072]{2,1,0:T(8,128)(2,1)} %dynamic-slice_bitcast_fusion), channel_id=1, source_target_pairs={{0,1},{1,0},{2,3},{3,2},{4,5},{5,4},{6,7},{7,6},{8,9},{9,8},{10,11... | collective-permute-start | bytes 4718600 | tf_op jit(solution)/shard_map/ppermute | solution.py:96
  153.3 3.7 %collective-permute-start.3 = (s32[2,512]{1,0:T(2,128)S(1)}, s32[2,512]{1,0:T(2,128)S(1)}, u32[]{:S(2)}, u32[]{:S(2)}) collective-permute-start(s32[2,512]{1,0:T(2,128)S(1)} %pad_add_fusion), channel_id=1, source_target_pairs={{0,4},{4,0},{8,12},{12,8},{16,20},{20,16},{24,28},{28,24},{1,5},{5... | collective-permute-start | bytes 12296 | tf_op jit(solution)/shard_map/ppermute | solution.py:172
  157.2 3.8 %copy-start.9 = (bf16[3072,1024]{1,0:T(8,128)(2,1)S(1)}, bf16[3072,1024]{1,0:T(8,128)(2,1)}, u32[]{:S(2)}) copy-start(bf16[3072,1024]{1,0:T(8,128)(2,1)} %all-gather.2.cloned.1.call-done) | copy-start | bytes 18874372
  159.5 19.3 %collective-permute-start.5 = (bf16[1,128,3072]{2,1,0:T(8,128)(2,1)S(1)}, bf16[1,128,3072]{2,1,0:T(8,128)(2,1)S(1)}, u32[]{:S(2)}, u32[]{:S(2)}) collective-permute-start(bf16[1,128,3072]{2,1,0:T(8,128)(2,1)S(1)} %constant_dynamic-slice_fusion), channel_id=1, source_target_pairs={{0,2},{1,3},{2,0},{3,1},{4,6},{5,7},{6,4},{7,5},{8,10},{9,11},{10,... | collective-permute-start | bytes 2359304 | tf_op jit(solution)/shard_map/ppermute | solution.py:96
  165.9 13.0 %copy-start.4 = (bf16[512,3072]{1,0:T(8,128)(2,1)}, bf16[512,3072]{1,0:T(8,128)(2,1)S(1)}, u32[]{:S(2)}) copy-start(bf16[512,3072]{1,0:T(8,128)(2,1)S(1)} %convolution_convert_fusion.3) | copy-start | bytes 9437188
  167.3 16.1 %collective-permute-start.1 = (bf16[2,128,3072]{2,1,0:T(8,128)(2,1)}, bf16[2,128,3072]{2,1,0:T(8,128)(2,1)}, u32[]{:S(2)}, u32[]{:S(2)}) collective-permute-start(bf16[2,128,3072]{2,1,0:T(8,128)(2,1)} %dynamic-slice_bitcast_fusion.1), channel_id=1, source_target_pairs={{0,1},{1,0},{2,3},{3,2},{4,5},{5,4},{6,7},{7,6},{8,9},{9,8},{10,11... | collective-permute-start | bytes 4718600 | tf_op jit(solution)/shard_map/ppermute | solution.py:96
  180.7 43.0 %all-to-all-start.3 = ((bf16[32,8,3200]{2,1,0:T(8,128)(2,1)}), bf16[32,8,3200]{2,1,0:T(8,128)(2,1)S(1)}, u32[]{:S(2)}, u32[]{:S(2)}) async-start(bf16[32,8,3200]{2,1,0:T(8,128)(2,1)} %fusion.1), calls=%async_computation.3 | async-start | bytes 3276800 | tf_op jit(solution)/shard_map/all_to_all | solution.py:208
  185.9 1.1 copy-start.2
  188.0 32.6 %collective-permute-start.2 = (bf16[1,128,3072]{2,1,0:T(8,128)(2,1)}, bf16[1,128,3072]{2,1,0:T(8,128)(2,1)S(1)}, u32[]{:S(2)}, u32[]{:S(2)}) collective-permute-start(bf16[1,128,3072]{2,1,0:T(8,128)(2,1)} %constant_dynamic-slice_fusion.2), channel_id=1, source_target_pairs={{0,2},{1,3},{2,0},{3,1},{4,6},{5,7},{6,4},{7,5},{8,10},{9,11},{10,... | collective-permute-start | bytes 2359304 | tf_op jit(solution)/shard_map/ppermute | solution.py:96
  223.7 44.5 %copy-start.1 = (bf16[32,8,3200]{2,1,0:T(8,128)(2,1)}, bf16[32,8,3200]{2,1,0:T(8,128)(2,1)S(1)}, u32[]{:S(2)}) copy-start(bf16[32,8,3200]{2,1,0:T(8,128)(2,1)S(1)} %all-to-all-done.3) | copy-start | bytes 4915204
  223.7 43.8 %all-to-all-start.2 = ((bf16[32,8,3200]{2,1,0:T(8,128)(2,1)}), bf16[32,8,3200]{2,1,0:T(8,128)(2,1)}, u32[]{:S(2)}, u32[]{:S(2)}) async-start(bf16[32,8,3200]{2,1,0:T(8,128)(2,1)} %fusion), calls=%async_computation.2 | async-start | bytes 3276800 | tf_op jit(solution)/shard_map/all_to_all | solution.py:208
Sparse Core Ops, SparseCore 0:
  8.9 134.7 all-gather.1

commit v3 on v1

--- a/solution.py
+++ b/solution.py
@@ -1,7 +1,10 @@
 import jax
 import jax.numpy as jnp
 from jax import lax
+from jax.experimental import pallas as pl
 from jax.sharding import PartitionSpec as P
+QUADS = 4
+
 
 def doc_of(positions, doc_ends):
     return jnp.sum((positions[:, None] >= doc_ends[None, :]).astype(jnp.int32), axis=1)
@@ -81,6 +84,49 @@
     slot = owners * capacity + jnp.sum(same.astype(jnp.int32), axis=1)
     slots = jnp.arange(owner_count * capacity, dtype=jnp.int32)
     return (slots[:, None] == slot[None, :]).astype(jnp.bfloat16)
+
+
+def head_sum(parts):
+    n_head = lax.axis_size("head")
+    head_rank = lax.axis_index("head")
+    step = 1
+    while step < n_head:
+        bit = (head_rank // step) % 2
+        pairs = parts.reshape((parts.shape[0] // 2, 2) + parts.shape[1:])
+        sent = lax.dynamic_index_in_dim(pairs, 1 - bit, axis=1, keepdims=False)
+        kept = lax.dynamic_index_in_dim(pairs, bit, axis=1, keepdims=False)
+        got = lax.ppermute(sent, "head", [(i, i ^ step) for i in range(n_head)])
+        parts = (kept.astype(jnp.float32) + got.astype(jnp.float32)).astype(jnp.bfloat16)
+        step *= 2
+    return parts[0]
+
+
+def merge_kernel(equal, *refs):
+    data, out = refs[:-1], refs[-1]
+    rows = jnp.concatenate([ref[...].reshape(-1, ref.shape[-1]) for ref in data], axis=0)
+    total = jnp.dot(equal[0], rows, preferred_element_type=jnp.float32)
+    out[...] = total.astype(out.dtype)
+
+
+def merged(equal, got, part):
+    n_hi, _, rows, _ = got[0].shape
+    width = part // n_hi
+    slots = equal.shape[1]
+    if width % 128 == 0 and rows % 16 == 0:
+        data = pl.BlockSpec((n_hi, 1, rows, width), lambda i, q: (0, q, 0, i))
+        return pl.pallas_call(
+            merge_kernel,
+            grid=(n_hi, QUADS),
+            in_specs=[pl.BlockSpec((1, slots, slots), lambda i, q: (q, 0, 0))] + [data] * QUADS,
+            out_specs=pl.BlockSpec((slots, width), lambda i, q: (0, QUADS * i + q)),
+            out_shape=jax.ShapeDtypeStruct((slots, QUADS * part), jnp.bfloat16),
+        )(equal, *got)
+    sets = []
+    for q in range(QUADS):
+        data = jnp.concatenate([g[:, q, :, :part].reshape(-1, part) for g in got], axis=0)
+        total = jnp.dot(equal[q], data, preferred_element_type=jnp.float32)
+        sets.append(total.astype(jnp.bfloat16).reshape(-1, n_hi, width))
+    return jnp.stack(sets, axis=2).reshape(slots, QUADS * part)
 
 
 def per_device(
@@ -96,7 +142,7 @@
     n_seq = lax.axis_size("seq")
     n_head = lax.axis_size("head")
     devices_all = n_seq * n_head
-    n_hi = n_seq // 2
+    n_hi = n_seq // QUADS
     tok_rows = queries.shape[0]
     head_local = decay_rate.shape[0]
     head_dim = queries.shape[1] // head_local
@@ -104,16 +150,25 @@
     head_rank = lax.axis_index("head")
     block_rows = tok_rows // n_head
     capacity = max(2, 2 * block_rows // devices_all)
-    swap = [(i, i ^ 1) for i in range(n_seq)]
-
-    stride = [[2 * i + low for i in range(n_hi)] for low in range(2)]
-    weights = lax.all_gather(
-        value_weight, "seq", axis=0, tiled=True, axis_index_groups=stride
-    )
-    half = weights.shape[0]
-
-    tags_own = jnp.stack([owner_block[:, 0], row_offset])
-    tags_pair = lax.ppermute(tags_own, "seq", swap)
+
+    def from_pair(array, k):
+        return lax.ppermute(array, "seq", [(i, i ^ k) for i in range(n_seq)])
+
+    if n_hi == 2:
+        there = from_pair(value_weight, QUADS)
+        is_low = seq_rank < QUADS
+        pieces = [(value_weight, there), (there, value_weight)]
+        weights = [jnp.where(is_low, a, b) for a, b in pieces]
+    else:
+        stride = [[QUADS * i + q for i in range(n_hi)] for q in range(QUADS)]
+        weights = [
+            lax.all_gather(value_weight, "seq", axis=0, tiled=True, axis_index_groups=stride)
+        ]
+    weights = jnp.concatenate(weights, axis=0)
+    width = weights.shape[0]
+
+    owners_own = owner_block[:, 0]
+    owners = [owners_own] + [from_pair(owners_own, k) for k in range(1, QUADS)]
 
     first_row = seq_rank * tok_rows
     positions = first_row + jnp.arange(tok_rows, dtype=jnp.int32)
@@ -133,52 +188,47 @@
     value_own = (
         (intra_part + inter_part).astype(jnp.bfloat16).reshape(tok_rows, head_local * head_dim)
     )
-    value_pair = lax.ppermute(value_own, "seq", swap)
-
-    def routed(value_rows, tags):
+    value_1 = from_pair(value_own, 1)
+    value_2 = from_pair(value_own, 2)
+    value_3 = from_pair(value_2, 1)
+
+    def routed(k, value_rows):
         part = lax.dot_general(
             value_rows, weights, (((1,), (1,)), ((), ())), preferred_element_type=jnp.float32
         ).astype(jnp.bfloat16)
-        parts = lax.all_to_all(
-            part.reshape(n_head, block_rows, half), "head", split_axis=0, concat_axis=0, tiled=True
+        rows = head_sum(part.reshape(n_head, block_rows, width))
+        start = head_rank * block_rows
+        places = slot_matrix(
+            lax.dynamic_slice_in_dim(owners[k], start, block_rows), capacity, devices_all
         )
-        rows = jnp.sum(parts.astype(jnp.float32), axis=0).astype(jnp.bfloat16)
-        mine = lax.dynamic_slice_in_dim(tags, head_rank * block_rows, block_rows, axis=1)
-        offsets = mine[1]
-        marks = jnp.stack([offsets // 64, offsets % 64, jnp.ones_like(offsets)], axis=1)
-        marks = jnp.pad(marks.astype(jnp.bfloat16), ((0, 0), (0, 125)))
-        places = slot_matrix(mine[0], capacity, devices_all)
-        sent = jnp.dot(
-            places, jnp.concatenate([rows, marks], axis=1), preferred_element_type=jnp.float32
-        ).astype(jnp.bfloat16)
+        if k == 0:
+            offsets = lax.dynamic_slice_in_dim(row_offset, start, block_rows)
+            marks = jnp.stack([offsets // 64, offsets % 64, jnp.ones_like(offsets)], axis=1)
+            marks = jnp.pad(marks.astype(jnp.bfloat16), ((0, 0), (0, 125)))
+            rows = jnp.concatenate([rows, marks], axis=1)
+        sent = jnp.dot(places, rows, preferred_element_type=jnp.float32).astype(jnp.bfloat16)
         got = lax.all_to_all(
-            sent.reshape(devices_all, capacity, half + 128),
+            sent.reshape(devices_all, capacity, rows.shape[1]),
             ("seq", "head"),
             split_axis=0,
             concat_axis=0,
             tiled=True,
         )
-        return got.reshape(n_hi, 2, n_head * capacity, half + 128)
-
-    got_own = routed(value_own, tags_own)
-    got_pair = routed(value_pair, tags_pair)
-
-    def marks_of(got, low):
-        return got[:, low, :, half:half + 3].astype(jnp.float32).reshape(-1, 3)
-
-    seen = [marks_of(got_own, 0), marks_of(got_pair, 0)]
-    keys = [jnp.where(m[:, 2] > 0, m[:, 0] * 64.0 + m[:, 1], -1.0) for m in seen]
-    whole = jnp.stack([k.reshape(n_hi, -1) for k in keys], axis=1).reshape(-1)
-    halves = []
-    for low in range(2):
-        total = 0.0
-        for got, key in ((got_own, keys[low]), (got_pair, keys[1 - low])):
-            equal = ((whole[:, None] == key[None, :]) & (whole >= 0)[:, None]).astype(jnp.bfloat16)
-            data = got[:, low, :, :half].reshape(-1, half)
-            total = total + jnp.dot(equal, data, preferred_element_type=jnp.float32)
-        halves.append(total.astype(jnp.bfloat16).reshape(-1, n_hi, half // n_hi))
-    row_grads = jnp.stack(halves, axis=2)
-    return row_grads.reshape(1, devices_all, capacity, 2 * half)
+        return got.reshape(n_hi, QUADS, n_head * capacity, rows.shape[1])
+
+    got = [routed(k, v) for k, v in enumerate((value_own, value_1, value_2, value_3))]
+    marks = got[0][..., width:width + 3].astype(jnp.float32)
+    keys = jnp.where(marks[..., 2] > 0, marks[..., 0] * 64.0 + marks[..., 1], -1.0)
+    whole = keys.reshape(-1, 1)
+    equal = jnp.stack([
+        (
+            (whole == jnp.concatenate([keys[:, q ^ k].reshape(-1) for k in range(QUADS)]))
+            & (whole >= 0)
+        ).astype(jnp.bfloat16)
+        for q in range(QUADS)
+    ])
+    row_grads = merged(equal, got, width)
+    return row_grads.reshape(1, devices_all, capacity, QUADS * width)
 
 
 def solution(mesh):

time: 365 us -> 264 us (0.72)
  waiting for transfers between devices: 235 us -> 152 us
  local copies, waits for them, and re-layouts: 31.1 us -> 10 us
  starting transfers between devices: 29.9 us -> 46.3 us
  between operations: 13.7 us -> 0.52 us
  matrix products: 32.5 us -> 24.9 us
  Pallas kernels: 0 us -> 7.34 us
    all_to_all x4, waiting for transfers between devices: 105 us -> 18.7 us  [routed(): lax.all_to_all(sent.reshape(devices_all, capacity, rows.shape[1]), ('seq'...]
    all_gather x1 -> x0, waiting for transfers between devices: 63.7 us -> none  [per_device(): lax.all_gather(value_weight, 'seq', axis=0, tiled=True, axis_index_groups...]
    ppermute x2 -> x15, waiting for transfers between devices: 25.8 us -> 66.5 us  [the longest x7 46.6 us: from_pair(): return lax.ppermute(array, 'seq', [(i, i ^ k) for i in range(n_seq)])]
    ppermute x2 -> x15, starting transfers between devices: 3.01 us -> 17.7 us  [the longest x7 11.3 us: from_pair(): return lax.ppermute(array, 'seq', [(i, i ^ k) for i in range(n_seq)])]
    all_to_all x1, waiting for transfers between devices: 9.84 us -> 23.7 us  [later_states(): back = lax.all_to_all(back, 'seq', split_axis=0, concat_axis=0, tiled=True)]
    all_to_all x1, waiting for transfers between devices: 29.8 us -> 43.5 us  [later_states(): got = lax.all_to_all(sent, 'seq', split_axis=0, concat_axis=0, tiled=True)]
    another operation x4, local copies, waits for them, and re-layouts: 14 us -> 0.32 us  [per_device(): keys[:, q ^ k].reshape(-1)]
    reshape x1 -> x0, local copies, waits for them, and re-layouts: 7.76 us -> none  [per_device(): return row_grads.reshape(1, devices_all, capacity, 2 * half)]
  transfers between devices with their start and end apart: 9 -> 21, of which waited for: 9 -> 12; matrix products, arithmetic and copies ran while one was open for 11% -> 16% of each run, Pallas kernels for 0% -> 0%
where the time goes in v3:
time: 264 us; the launch traced here: 263 us
  waiting for transfers between devices  152 us (58%)
  starting transfers between devices  46.3 us (18%)
  matrix products  24.9 us (9%)
  other arithmetic  21.3 us (8%)
  local copies, waits for them, and re-layouts  10 us (4%)
  Pallas kernels  7.34 us (3%)
    ppermute x7, waiting for transfers between devices, from_pair(): return lax.ppermute(array, 'seq', [(i, i ^ k) for i in range(n_seq)])  46.6 us
    all_to_all x1, waiting for transfers between devices, later_states(): got = lax.all_to_all(sent, 'seq', split_axis=0, concat_axis=0, tiled=True)  43.5 us
    all_to_all x1, waiting for transfers between devices, later_states(): back = lax.all_to_all(back, 'seq', split_axis=0, concat_axis=0, tiled=True)  23.7 us
    ppermute x8, waiting for transfers between devices, head_sum(): got = lax.ppermute(sent, 'head', [(i, i ^ step) for i in range(n_head)])  19.9 us
    all_to_all x4, waiting for transfers between devices, routed(): lax.all_to_all(sent.reshape(devices_all, capacity, rows.shape[1]), ('seq'...  18.7 us
    all_to_all x4, starting transfers between devices, routed(): lax.all_to_all(sent.reshape(devices_all, capacity, rows.shape[1]), ('seq'...  17.9 us
    dot_general x4, matrix products, routed(): lax.dot_general(value_rows, weights, (((1,), (1,)), ((), ())), preferred_...  12.5 us
    ppermute x7, starting transfers between devices, from_pair(): return lax.ppermute(array, 'seq', [(i, i ^ k) for i in range(n_seq)])  11.3 us
  transfers between devices with their start and end apart: 21, of which 12 were waited for; matrix products, arithmetic and copies ran while one was open for 16% of the time, Pallas kernels for 0%

profile of v3, /device:TPU:0, one launch (start us, length us, event | category | flops | bytes accessed | tf_op | source)
XLA Modules:
  0.0 262.9 jit_solution(11244089340938012203)
XLA Ops:
  4.1 1.5 copy.31
  5.7 1.3 broadcast_compare_fusion
  7.0 1.3 fusion.15
  8.3 7.3 %all-to-all-start = ((f32[8,128,128]{2,1,0:T(8,128)}), f32[8,128,128]{2,1,0:T(8,128)S(1)}, u32[]{:S(2)}, u32[]{:S(2)}) async-start(f32[8,128,128]{2,1,0:T(8,128)} %fusion.15), calls=%async_computation | async-start | bytes 1048576 | tf_op jit(solution)/shard_map/all_to_all | solution.py:61
  15.6 2.9 %collective-permute-start = (bf16[768,1024]{1,0:T(8,128)(2,1)}, bf16[768,1024]{1,0:T(8,128)(2,1)}, u32[]{:S(2)}, u32[]{:S(2)}) collective-permute-start(bf16[768,1024]{1,0:T(8,128)(2,1)} %param.11), channel_id=1, source_target_pairs={{0,16},{4,20},{8,24},{12,28},{16,0},{20,4},{24,8},{28,12},{1,17},{... | collective-permute-start | bytes 4718600 | tf_op jit(solution)/shard_map/ppermute | solution.py:155
  19.6 1.0 fusion.22
  20.6 1.2 fusion.14
  21.7 43.5 %all-to-all-done = f32[8,128,128]{2,1,0:T(8,128)S(1)} async-done(((f32[8,128,128]{2,1,0:T(8,128)}), f32[8,128,128]{2,1,0:T(8,128)S(1)}, u32[]{:S(2)}, u32[]{:S(2)}) %all-to-all-start) | async-done | bytes 524320 | tf_op jit(solution)/shard_map/all_to_all | solution.py:61
  70.6 3.4 %all-to-all-start.1 = ((bf16[8,128,128]{2,1,0:T(8,128)(2,1)}), bf16[8,128,128]{2,1,0:T(8,128)(2,1)S(1)}, u32[]{:S(2)}, u32[]{:S(2)}) async-start(bf16[8,128,128]{2,1,0:T(8,128)(2,1)} %constant_dynamic-update-slice_fusion), calls=%async_computation.1 | async-start | bytes 524288 | tf_op jit(solution)/shard_map/all_to_all | solution.py:76
  74.0 5.4 %fusion = f32[8,512,128]{1,2,0:T(8,128)S(1)} fusion(f32[512,512]{1,0:T(8,128)} %fusion.14, f32[8]{0:T(128)S(1)} %get-tuple-element.39, pred[512,512]{1,0:T(8,128)(4,1)} %fusion.22, bf16[512,8,128]{0,2,1:T(8,128)(2,1)} %bitcast.137, bf16[512,1024]{1,0:T(8,128)(2,1)} %param.10, bf16[512,1024]{1,0:T(8,128)(2,1)S(1)} %copy-done), kind=kOutput, calls=%fused_computation.1 | convolution fusion | flops 1084227584 | bytes 6553632 | tf_op jit(solution)/shard_map/hst,thf->shf/dot_general | solution.py:24
  79.5 23.7 %all-to-all-done.1 = bf16[8,128,128]{2,1,0:T(8,128)(2,1)S(1)} async-done(((bf16[8,128,128]{2,1,0:T(8,128)(2,1)}), bf16[8,128,128]{2,1,0:T(8,128)(2,1)S(1)}, u32[]{:S(2)}, u32[]{:S(2)}) %all-to-all-start.1) | async-done | bytes 262176 | tf_op jit(solution)/shard_map/all_to_all | solution.py:76
  103.7 2.5 broadcast_select_fusion.1
  106.3 1.8 convolution_convert_fusion.3
  109.5 1.1 collective-permute-start.8
  111.8 1.6 collective-permute-start.2
  113.4 22.0 %collective-permute-done.8 = bf16[512,1024]{0,1:T(8,128)(2,1)} collective-permute-done((bf16[512,1024]{0,1:T(8,128)(2,1)}, bf16[512,1024]{0,1:T(8,128)(2,1)}, u32[]{:S(2)}, u32[]{:S(2)}) %collective-permute-start.8) | collective-permute-done | bytes 1048608 | tf_op jit(solution)/shard_map/ppermute | solution.py:155
  135.4 3.1 %convolution_convert_fusion.1 = bf16[512,1536]{1,0:T(8,128)(2,1)S(1)} fusion(bf16[512,1024]{0,1:T(8,128)(2,1)} %collective-permute-done.8, bf16[768,1024]{1,0:T(8,128)(2,1)S(1)} %copy-done.11, bf16[768,1024]{1,0:T(8,128)(2,1)S(1)} %copy-done.8), kind=kOutput, calls=%fused_computation.6 | convolution fusion | flops 1617690624 | bytes 5767168 | tf_op jit(solution)/shard_map/dot_general | solution.py:196
  139.5 1.3 fusion.4
  140.9 3.9 %all-to-all-start.2 = ((bf16[32,8,1664]{2,1,0:T(8,128)(2,1)}), bf16[32,8,1664]{2,1,0:T(8,128)(2,1)S(1)}, u32[]{:S(2)}, u32[]{:S(2)}) async-start(bf16[32,8,1664]{2,1,0:T(8,128)(2,1)} %fusion.4), calls=%async_computation.2 | async-start | bytes 1703936 | tf_op jit(solution)/shard_map/all_to_all | solution.py:210
  144.7 4.0 %convolution_convert_fusion.2 = bf16[512,1536]{1,0:T(8,128)(2,1)S(1)} fusion(bf16[512,1024]{0,1:T(8,128)(2,1)} %collective-permute-done.4, bf16[768,1024]{1,0:T(8,128)(2,1)} %copy-done.10, bf16[768,1024]{1,0:T(8,128)(2,1)} %copy-done.7), kind=kOutput, calls=%fused_computation.7 | convolution fusion | flops 1617690624 | bytes 5767168 | tf_op jit(solution)/shard_map/dot_general | solution.py:196
  148.8 1.1 dynamic-slice_bitcast_fusion.2
  150.0 1.7 collective-permute-start.12
  151.7 1.3 fusion.11
  153.0 1.5 collective-permute-start.10
  154.6 1.5 collective-permute-start.7
  156.0 3.0 %collective-permute-done.7 = s32[512]{0:T(512)S(1)} collective-permute-done((s32[512]{0:T(512)S(1)}, s32[512]{0:T(512)S(1)}, u32[]{:S(2)}, u32[]{:S(2)}) %collective-permute-start.7) | collective-permute-done | bytes 2080 | tf_op jit(solution)/shard_map/ppermute | solution.py:155
  159.3 7.7 %collective-permute-done.10 = bf16[1,128,1536]{2,1,0:T(8,128)(2,1)S(1)} collective-permute-done((bf16[1,128,1536]{2,1,0:T(8,128)(2,1)S(1)}, bf16[1,128,1536]{2,1,0:T(8,128)(2,1)S(1)}, u32[]{:S(2)}, u32[]{:S(2)}) %collective-permute-start.10) | collective-permute-done | bytes 393248 | tf_op jit(solution)/shard_map/ppermute | solution.py:98
  167.0 1.3 fusion.6
  168.3 4.3 %all-to-all-start.4 = ((bf16[32,8,1536]{2,1,0:T(8,128)(2,1)}), bf16[32,8,1536]{2,1,0:T(8,128)(2,1)S(1)}, u32[]{:S(2)}, u32[]{:S(2)}) async-start(bf16[32,8,1536]{2,1,0:T(8,128)(2,1)} %fusion.6), calls=%async_computation.4 | async-start | bytes 1572864 | tf_op jit(solution)/shard_map/all_to_all | solution.py:210
  172.6 1.7 fusion.12
  174.3 11.7 %collective-permute-done.12 = bf16[512,1024]{0,1:T(8,128)(2,1)} collective-permute-done((bf16[512,1024]{0,1:T(8,128)(2,1)}, bf16[512,1024]{0,1:T(8,128)(2,1)}, u32[]{:S(2)}, u32[]{:S(2)}) %collective-permute-start.12) | collective-permute-done | bytes 1048608 | tf_op jit(solution)/shard_map/ppermute | solution.py:155
  186.1 3.6 %convolution_convert_fusion = bf16[512,1536]{1,0:T(8,128)(2,1)S(1)} fusion(bf16[512,1024]{0,1:T(8,128)(2,1)} %collective-permute-done.12, bf16[768,1024]{1,0:T(8,128)(2,1)} %copy-done.10, bf16[768,1024]{1,0:T(8,128)(2,1)S(1)} %copy-done.9), kind=kOutput, calls=%fused_computation.5 | convolution fusion | flops 1617690624 | bytes 5767168 | tf_op jit(solution)/shard_map/dot_general | solution.py:196
  189.6 1.0 dynamic-slice_bitcast_fusion
  190.7 1.4 collective-permute-start.6
  192.1 1.3 collective-permute-start.3
  193.4 2.3 collective-permute-done.3
  196.0 6.3 %collective-permute-done.6 = bf16[1,128,1536]{2,1,0:T(8,128)(2,1)S(1)} collective-permute-done((bf16[1,128,1536]{2,1,0:T(8,128)(2,1)S(1)}, bf16[1,128,1536]{2,1,0:T(8,128)(2,1)S(1)}, u32[]{:S(2)}, u32[]{:S(2)}) %collective-permute-start.6) | collective-permute-done | bytes 393248 | tf_op jit(solution)/shard_map/ppermute | solution.py:98
  202.3 1.3 fusion.5
  203.6 4.8 %all-to-all-start.3 = ((bf16[32,8,1536]{2,1,0:T(8,128)(2,1)}), bf16[32,8,1536]{2,1,0:T(8,128)(2,1)S(1)}, u32[]{:S(2)}, u32[]{:S(2)}) async-start(bf16[32,8,1536]{2,1,0:T(8,128)(2,1)} %fusion.5), calls=%async_computation.3 | async-start | bytes 1572864 | tf_op jit(solution)/shard_map/all_to_all | solution.py:210
  208.5 1.6 fusion.10
  210.1 1.8 collective-permute-start.14
  211.9 2.4 collective-permute-start.11
  214.3 7.6 %collective-permute-done.11 = s32[512]{0:T(512)S(1)} collective-permute-done((s32[512]{0:T(512)S(1)}, s32[512]{0:T(512)S(1)}, u32[]{:S(2)}, u32[]{:S(2)}) %collective-permute-start.11) | collective-permute-done | bytes 2080 | tf_op jit(solution)/shard_map/ppermute | solution.py:155
  222.2 5.7 %collective-permute-done.14 = bf16[1,128,1536]{2,1,0:T(8,128)(2,1)S(1)} collective-permute-done((bf16[1,128,1536]{2,1,0:T(8,128)(2,1)S(1)}, bf16[1,128,1536]{2,1,0:T(8,128)(2,1)S(1)}, u32[]{:S(2)}, u32[]{:S(2)}) %collective-permute-start.14) | collective-permute-done | bytes 393248 | tf_op jit(solution)/shard_map/ppermute | solution.py:98
  227.9 1.3 fusion.7
  229.2 4.9 %all-to-all-start.5 = ((bf16[32,8,1536]{2,1,0:T(8,128)(2,1)}), bf16[32,8,1536]{2,1,0:T(8,128)(2,1)S(1)}, u32[]{:S(2)}, u32[]{:S(2)}) async-start(bf16[32,8,1536]{2,1,0:T(8,128)(2,1)} %fusion.7), calls=%async_computation.5 | async-start | bytes 1572864 | tf_op jit(solution)/shard_map/all_to_all | solution.py:210
  236.0 18.7 %all-to-all-done.5 = bf16[32,8,1536]{2,1,0:T(8,128)(2,1)S(1)} async-done(((bf16[32,8,1536]{2,1,0:T(8,128)(2,1)}), bf16[32,8,1536]{2,1,0:T(8,128)(2,1)S(1)}, u32[]{:S(2)}, u32[]{:S(2)}) %all-to-all-start.5) | async-done | bytes 786464 | tf_op jit(solution)/shard_map/all_to_all | solution.py:210
  255.5 7.3 %shard_map.82 = bf16[256,6144]{1,0:T(8,128)(2,1)} custom-call(bf16[4,256,256]{2,1,0:T(8,128)(2,1)} %add_convert_fusion.equal, bf16[2,4,32,1664]{3,2,1,0:T(8,128)(2,1)} %bitcast.121, bf16[2,4,32,1536]{3,2,1,0:T(8,128)(2,1)} %bitcast.123, bf16[2,4,32,1536]{3,2,1,0:T(8,128)(2,1)} %bitcast.122, bf16[2,4,32,1536]{3,2,1,0:T(8,128)(2,1)} %bitcast.124), custom_call_target="tpu_custom_call" | custom-call | tf_op jit(solution)/shard_map/pallas_call | solution.py:117
  (109 shorter events, 18.6 us)
Async XLA Ops:
  0.0 74.0 %copy-start = (bf16[512,1024]{1,0:T(8,128)(2,1)S(1)}, bf16[512,1024]{1,0:T(8,128)(2,1)}, u32[]{:S(2)}) copy-start(bf16[512,1024]{1,0:T(8,128)(2,1)} %param.9) | copy-start | bytes 3145732
  0.0 7.0 %copy-start.15 = (bf16[512,1024]{1,0:T(8,128)(2,1)S(1)}, bf16[512,1024]{1,0:T(8,128)(2,1)}, u32[]{:S(2)}) copy-start(bf16[512,1024]{1,0:T(8,128)(2,1)} %param.10) | copy-start | bytes 3145732
  5.6 2.7 %copy-start.13 = (bf16[512,1024]{0,1:T(8,128)(2,1)}, bf16[512,1024]{0,1:T(8,128)(2,1)S(1)}, u32[]{:S(2)}) copy-start(bf16[512,1024]{0,1:T(8,128)(2,1)S(1)} %copy.31) | copy-start | bytes 3145732
  8.3 56.9 %all-to-all-start = ((f32[8,128,128]{2,1,0:T(8,128)}), f32[8,128,128]{2,1,0:T(8,128)S(1)}, u32[]{:S(2)}, u32[]{:S(2)}) async-start(f32[8,128,128]{2,1,0:T(8,128)} %fusion.15), calls=%async_computation | async-start | bytes 1048576 | tf_op jit(solution)/shard_map/all_to_all | solution.py:61
  15.6 88.1 %collective-permute-start = (bf16[768,1024]{1,0:T(8,128)(2,1)}, bf16[768,1024]{1,0:T(8,128)(2,1)}, u32[]{:S(2)}, u32[]{:S(2)}) collective-permute-start(bf16[768,1024]{1,0:T(8,128)(2,1)} %param.11), channel_id=1, source_target_pairs={{0,16},{4,20},{8,24},{12,28},{16,0},{20,4},{24,8},{28,12},{1,17},{... | collective-permute-start | bytes 4718600 | tf_op jit(solution)/shard_map/ppermute | solution.py:155
  70.6 32.6 %all-to-all-start.1 = ((bf16[8,128,128]{2,1,0:T(8,128)(2,1)}), bf16[8,128,128]{2,1,0:T(8,128)(2,1)S(1)}, u32[]{:S(2)}, u32[]{:S(2)}) async-start(bf16[8,128,128]{2,1,0:T(8,128)(2,1)} %constant_dynamic-update-slice_fusion), calls=%async_computation.1 | async-start | bytes 524288 | tf_op jit(solution)/shard_map/all_to_all | solution.py:76
  103.7 2.5 copy-start.12
  106.2 1.9 copy-start.7
  106.2 1.9 copy-start.10
  106.2 3.2 %copy-start.14 = (s32[512,1]{0,1:T(1,128)S(1)}, s32[512,1]{0,1:T(1,128)}, u32[]{:S(2)}) copy-start(s32[512,1]{0,1:T(1,128)} %param.14) | copy-start | bytes 6148
  109.1 2.5 collective-permute-start.1
  109.5 26.0 %copy-start.8 = (bf16[768,1024]{1,0:T(8,128)(2,1)S(1)}, bf16[768,1024]{1,0:T(8,128)(2,1)}, u32[]{:S(2)}) copy-start(bf16[768,1024]{1,0:T(8,128)(2,1)} %copy-done.7) | copy-start | bytes 4718596
  109.5 25.9 %copy-start.11 = (bf16[768,1024]{1,0:T(8,128)(2,1)S(1)}, bf16[768,1024]{1,0:T(8,128)(2,1)}, u32[]{:S(2)}) copy-start(bf16[768,1024]{1,0:T(8,128)(2,1)} %copy-done.10) | copy-start | bytes 4718596
  109.5 25.9 %collective-permute-start.8 = (bf16[512,1024]{0,1:T(8,128)(2,1)}, bf16[512,1024]{0,1:T(8,128)(2,1)}, u32[]{:S(2)}, u32[]{:S(2)}) collective-permute-start(bf16[512,1024]{0,1:T(8,128)(2,1)} %bitcast.134), channel_id=1, source_target_pairs={{0,8},{4,12},{8,0},{12,4},{16,24},{20,28},{24,16},{28,20},{1,9},{5... | collective-permute-start | bytes 3145736 | tf_op jit(solution)/shard_map/ppermute | solution.py:155
  110.8 33.9 %collective-permute-start.4 = (bf16[512,1024]{0,1:T(8,128)(2,1)}, bf16[512,1024]{0,1:T(8,128)(2,1)}, u32[]{:S(2)}, u32[]{:S(2)}) collective-permute-start(bf16[512,1024]{0,1:T(8,128)(2,1)} %bitcast.135), channel_id=1, source_target_pairs={{0,4},{4,0},{8,12},{12,8},{16,20},{20,16},{24,28},{28,24},{1,5},{5... | collective-permute-start | bytes 3145736 | tf_op jit(solution)/shard_map/ppermute | solution.py:155
  111.8 27.6 %collective-permute-start.2 = (bf16[1,128,1536]{2,1,0:T(8,128)(2,1)S(1)}, bf16[1,128,1536]{2,1,0:T(8,128)(2,1)S(1)}, u32[]{:S(2)}, u32[]{:S(2)}) collective-permute-start(bf16[1,128,1536]{2,1,0:T(8,128)(2,1)S(1)} %constant_dynamic-slice_fusion.3), channel_id=1, source_target_pairs={{0,2},{1,3},{2,0},{3,1},{4,6},{5,7},{6,4},{7,5},{8,10},{9,11},{10,... | collective-permute-start | bytes 1179656 | tf_op jit(solution)/shard_map/ppermute | solution.py:98
  139.4 12.2 %collective-permute-start.9 = (bf16[2,128,1536]{2,1,0:T(8,128)(2,1)}, bf16[2,128,1536]{2,1,0:T(8,128)(2,1)}, u32[]{:S(2)}, u32[]{:S(2)}) collective-permute-start(bf16[2,128,1536]{2,1,0:T(8,128)(2,1)} %dynamic-slice_bitcast_fusion.1), channel_id=1, source_target_pairs={{0,1},{1,0},{2,3},{3,2},{4,5},{5,4},{6,7},{7,6},{8,9},{9,8},{10,11... | collective-permute-start | bytes 2359304 | tf_op jit(solution)/shard_map/ppermute | solution.py:98
  140.9 27.4 %all-to-all-start.2 = ((bf16[32,8,1664]{2,1,0:T(8,128)(2,1)}), bf16[32,8,1664]{2,1,0:T(8,128)(2,1)S(1)}, u32[]{:S(2)}, u32[]{:S(2)}) async-start(bf16[32,8,1664]{2,1,0:T(8,128)(2,1)} %fusion.4), calls=%async_computation.2 | async-start | bytes 1703936 | tf_op jit(solution)/shard_map/all_to_all | solution.py:210
  148.8 4.2 %copy-start.5 = (bf16[512,1536]{1,0:T(8,128)(2,1)}, bf16[512,1536]{1,0:T(8,128)(2,1)S(1)}, u32[]{:S(2)}) copy-start(bf16[512,1536]{1,0:T(8,128)(2,1)S(1)} %convolution_convert_fusion.2) | copy-start | bytes 4718596
  149.9 22.7 %collective-permute-start.5 = (bf16[2,128,1536]{2,1,0:T(8,128)(2,1)}, bf16[2,128,1536]{2,1,0:T(8,128)(2,1)}, u32[]{:S(2)}, u32[]{:S(2)}) collective-permute-start(bf16[2,128,1536]{2,1,0:T(8,128)(2,1)} %dynamic-slice_bitcast_fusion.2), channel_id=1, source_target_pairs={{0,1},{1,0},{2,3},{3,2},{4,5},{5,4},{6,7},{7,6},{8,9},{9,8},{10,11... | collective-permute-start | bytes 2359304 | tf_op jit(solution)/shard_map/ppermute | solution.py:98
  150.0 36.1 %collective-permute-start.12 = (bf16[512,1024]{0,1:T(8,128)(2,1)}, bf16[512,1024]{0,1:T(8,128)(2,1)}, u32[]{:S(2)}, u32[]{:S(2)}) collective-permute-start(bf16[512,1024]{0,1:T(8,128)(2,1)} %collective-permute-done.8), channel_id=1, source_target_pairs={{0,4},{4,0},{8,12},{12,8},{16,20},{20,16},{24,28},{28,24},{1,5},{5... | collective-permute-start | bytes 3145736 | tf_op jit(solution)/shard_map/ppermute | solution.py:155
  153.0 14.0 %collective-permute-start.10 = (bf16[1,128,1536]{2,1,0:T(8,128)(2,1)S(1)}, bf16[1,128,1536]{2,1,0:T(8,128)(2,1)S(1)}, u32[]{:S(2)}, u32[]{:S(2)}) collective-permute-start(bf16[1,128,1536]{2,1,0:T(8,128)(2,1)S(1)} %constant_dynamic-slice_fusion.1), channel_id=1, source_target_pairs={{0,2},{1,3},{2,0},{3,1},{4,6},{5,7},{6,4},{7,5},{8,10},{9,11},{10,... | collective-permute-start | bytes 1179656 | tf_op jit(solution)/shard_map/ppermute | solution.py:98
  154.6 4.4 %collective-permute-start.7 = (s32[512]{0:T(512)S(1)}, s32[512]{0:T(512)S(1)}, u32[]{:S(2)}, u32[]{:S(2)}) collective-permute-start(s32[512]{0:T(512)S(1)} %bitcast.140), channel_id=1, source_target_pairs={{0,8},{4,12},{8,0},{12,4},{16,24},{20,28},{24,16},{28,20},{1,9},{5... | collective-permute-start | bytes 6152 | tf_op jit(solution)/shard_map/ppermute | solution.py:155
  168.3 65.8 %copy-start.1 = (bf16[32,8,1664]{2,1,0:T(8,128)(2,1)}, bf16[32,8,1664]{2,1,0:T(8,128)(2,1)S(1)}, u32[]{:S(2)}) copy-start(bf16[32,8,1664]{2,1,0:T(8,128)(2,1)S(1)} %all-to-all-done.2) | copy-start | bytes 2555908
  168.3 35.4 %all-to-all-start.4 = ((bf16[32,8,1536]{2,1,0:T(8,128)(2,1)}), bf16[32,8,1536]{2,1,0:T(8,128)(2,1)S(1)}, u32[]{:S(2)}, u32[]{:S(2)}) async-start(bf16[32,8,1536]{2,1,0:T(8,128)(2,1)} %fusion.6), calls=%async_computation.4 | async-start | bytes 1572864 | tf_op jit(solution)/shard_map/all_to_all | solution.py:210
  172.6 13.4 %copy-start.9 = (bf16[768,1024]{1,0:T(8,128)(2,1)S(1)}, bf16[768,1024]{1,0:T(8,128)(2,1)}, u32[]{:S(2)}) copy-start(bf16[768,1024]{1,0:T(8,128)(2,1)} %copy-done.7) | copy-start | bytes 4718596
  189.6 12.7 %copy-start.6 = (bf16[512,1536]{1,0:T(8,128)(2,1)}, bf16[512,1536]{1,0:T(8,128)(2,1)S(1)}, u32[]{:S(2)}) copy-start(bf16[512,1536]{1,0:T(8,128)(2,1)S(1)} %convolution_convert_fusion) | copy-start | bytes 4718596
  190.7 17.8 %collective-permute-start.13 = (bf16[2,128,1536]{2,1,0:T(8,128)(2,1)}, bf16[2,128,1536]{2,1,0:T(8,128)(2,1)}, u32[]{:S(2)}, u32[]{:S(2)}) collective-permute-start(bf16[2,128,1536]{2,1,0:T(8,128)(2,1)} %dynamic-slice_bitcast_fusion), channel_id=1, source_target_pairs={{0,1},{1,0},{2,3},{3,2},{4,5},{5,4},{6,7},{7,6},{8,9},{9,8},{10,11... | collective-permute-start | bytes 2359304 | tf_op jit(solution)/shard_map/ppermute | solution.py:98
  190.7 11.6 %collective-permute-start.6 = (bf16[1,128,1536]{2,1,0:T(8,128)(2,1)S(1)}, bf16[1,128,1536]{2,1,0:T(8,128)(2,1)S(1)}, u32[]{:S(2)}, u32[]{:S(2)}) collective-permute-start(bf16[1,128,1536]{2,1,0:T(8,128)(2,1)S(1)} %constant_dynamic-slice_fusion.2), channel_id=1, source_target_pairs={{0,2},{1,3},{2,0},{3,1},{4,6},{5,7},{6,4},{7,5},{8,10},{9,11},{10,... | collective-permute-start | bytes 1179656 | tf_op jit(solution)/shard_map/ppermute | solution.py:98
  192.1 3.6 %collective-permute-start.3 = (s32[512]{0:T(512)S(1)}, s32[512]{0:T(512)S(1)}, u32[]{:S(2)}, u32[]{:S(2)}) collective-permute-start(s32[512]{0:T(512)S(1)} %bitcast.141), channel_id=1, source_target_pairs={{0,4},{4,0},{8,12},{12,8},{16,20},{20,16},{24,28},{28,24},{1,5},{5... | collective-permute-start | bytes 6152 | tf_op jit(solution)/shard_map/ppermute | solution.py:155
  203.6 6.5 %copy-start.2 = (bf16[32,8,1536]{2,1,0:T(8,128)(2,1)}, bf16[32,8,1536]{2,1,0:T(8,128)(2,1)S(1)}, u32[]{:S(2)}) copy-start(bf16[32,8,1536]{2,1,0:T(8,128)(2,1)S(1)} %all-to-all-done.4) | copy-start | bytes 2359300
  203.6 25.5 %all-to-all-start.3 = ((bf16[32,8,1536]{2,1,0:T(8,128)(2,1)}), bf16[32,8,1536]{2,1,0:T(8,128)(2,1)S(1)}, u32[]{:S(2)}, u32[]{:S(2)}) async-start(bf16[32,8,1536]{2,1,0:T(8,128)(2,1)} %fusion.5), calls=%async_computation.3 | async-start | bytes 1572864 | tf_op jit(solution)/shard_map/all_to_all | solution.py:210
  210.1 17.8 %collective-permute-start.14 = (bf16[1,128,1536]{2,1,0:T(8,128)(2,1)S(1)}, bf16[1,128,1536]{2,1,0:T(8,128)(2,1)S(1)}, u32[]{:S(2)}, u32[]{:S(2)}) collective-permute-start(bf16[1,128,1536]{2,1,0:T(8,128)(2,1)S(1)} %constant_dynamic-slice_fusion), channel_id=1, source_target_pairs={{0,2},{1,3},{2,0},{3,1},{4,6},{5,7},{6,4},{7,5},{8,10},{9,11},{10,... | collective-permute-start | bytes 1179656 | tf_op jit(solution)/shard_map/ppermute | solution.py:98
  211.9 10.0 %collective-permute-start.11 = (s32[512]{0:T(512)S(1)}, s32[512]{0:T(512)S(1)}, u32[]{:S(2)}, u32[]{:S(2)}) collective-permute-start(s32[512]{0:T(512)S(1)} %bitcast.142), channel_id=1, source_target_pairs={{0,12},{4,8},{8,4},{12,0},{16,28},{20,24},{24,20},{28,16},{1,13},{... | collective-permute-start | bytes 6152 | tf_op jit(solution)/shard_map/ppermute | solution.py:155
  229.2 25.5 %copy-start.3 = (bf16[32,8,1536]{2,1,0:T(8,128)(2,1)}, bf16[32,8,1536]{2,1,0:T(8,128)(2,1)S(1)}, u32[]{:S(2)}) copy-start(bf16[32,8,1536]{2,1,0:T(8,128)(2,1)S(1)} %all-to-all-done.3) | copy-start | bytes 2359300
  229.2 25.5 %all-to-all-start.5 = ((bf16[32,8,1536]{2,1,0:T(8,128)(2,1)}), bf16[32,8,1536]{2,1,0:T(8,128)(2,1)S(1)}, u32[]{:S(2)}, u32[]{:S(2)}) async-start(bf16[32,8,1536]{2,1,0:T(8,128)(2,1)} %fusion.7), calls=%async_computation.5 | async-start | bytes 1572864 | tf_op jit(solution)/shard_map/all_to_all | solution.py:210
  254.7 0.9 copy-start.4

commit v4 on v3

--- a/solution.py
+++ b/solution.py
@@ -109,24 +109,29 @@
 
 
 def merged(equal, got, part):
-    n_hi, _, rows, _ = got[0].shape
-    width = part // n_hi
+    _, n_mid, _, rows, _ = got[0].shape
+    width = part // n_mid
     slots = equal.shape[1]
     if width % 128 == 0 and rows % 16 == 0:
-        data = pl.BlockSpec((n_hi, 1, rows, width), lambda i, q: (0, q, 0, i))
+        data = pl.BlockSpec((1, n_mid, 1, rows, width), lambda t, i, u: (t, 0, u, 0, i))
         return pl.pallas_call(
             merge_kernel,
-            grid=(n_hi, QUADS),
-            in_specs=[pl.BlockSpec((1, slots, slots), lambda i, q: (q, 0, 0))] + [data] * QUADS,
-            out_specs=pl.BlockSpec((slots, width), lambda i, q: (0, QUADS * i + q)),
+            grid=(2, n_mid, 2),
+            in_specs=[pl.BlockSpec((1, slots, slots), lambda t, i, u: (2 * t + u, 0, 0))]
+            + [data] * QUADS,
+            out_specs=pl.BlockSpec(
+                (slots, width), lambda t, i, u: (0, (t * n_mid + i) * 2 + u)
+            ),
             out_shape=jax.ShapeDtypeStruct((slots, QUADS * part), jnp.bfloat16),
         )(equal, *got)
     sets = []
-    for q in range(QUADS):
-        data = jnp.concatenate([g[:, q, :, :part].reshape(-1, part) for g in got], axis=0)
-        total = jnp.dot(equal[q], data, preferred_element_type=jnp.float32)
-        sets.append(total.astype(jnp.bfloat16).reshape(-1, n_hi, width))
-    return jnp.stack(sets, axis=2).reshape(slots, QUADS * part)
+    for t in range(2):
+        for u in range(2):
+            data = jnp.concatenate([g[t, :, u, :, :part].reshape(-1, part) for g in got], axis=0)
+            total = jnp.dot(equal[2 * t + u], data, preferred_element_type=jnp.float32)
+            sets.append(total.astype(jnp.bfloat16).reshape(-1, n_mid, width))
+    sides = [jnp.stack(sets[2 * t:2 * t + 2], axis=2) for t in range(2)]
+    return jnp.stack(sides, axis=1).reshape(slots, QUADS * part)
 
 
 def per_device(
@@ -142,7 +147,8 @@
     n_seq = lax.axis_size("seq")
     n_head = lax.axis_size("head")
     devices_all = n_seq * n_head
-    n_hi = n_seq // QUADS
+    n_mid = n_seq // QUADS
+    top = n_seq // 2
     tok_rows = queries.shape[0]
     head_local = decay_rate.shape[0]
     head_dim = queries.shape[1] // head_local
@@ -154,21 +160,21 @@
     def from_pair(array, k):
         return lax.ppermute(array, "seq", [(i, i ^ k) for i in range(n_seq)])
 
-    if n_hi == 2:
-        there = from_pair(value_weight, QUADS)
-        is_low = seq_rank < QUADS
+    if n_mid == 2:
+        there = from_pair(value_weight, 2)
+        is_low = (seq_rank // 2) % 2 == 0
         pieces = [(value_weight, there), (there, value_weight)]
         weights = [jnp.where(is_low, a, b) for a, b in pieces]
     else:
-        stride = [[QUADS * i + q for i in range(n_hi)] for q in range(QUADS)]
+        groups = [[t * top + 2 * m + u for m in range(n_mid)] for t in range(2) for u in range(2)]
         weights = [
-            lax.all_gather(value_weight, "seq", axis=0, tiled=True, axis_index_groups=stride)
+            lax.all_gather(value_weight, "seq", axis=0, tiled=True, axis_index_groups=groups)
         ]
     weights = jnp.concatenate(weights, axis=0)
     width = weights.shape[0]
 
     owners_own = owner_block[:, 0]
-    owners = [owners_own] + [from_pair(owners_own, k) for k in range(1, QUADS)]
+    owners = [owners_own] + [from_pair(owners_own, k) for k in (1, top, top + 1)]
 
     first_row = seq_rank * tok_rows
     positions = first_row + jnp.arange(tok_rows, dtype=jnp.int32)
@@ -188,15 +194,17 @@
     value_own = (
         (intra_part + inter_part).astype(jnp.bfloat16).reshape(tok_rows, head_local * head_dim)
     )
-    value_1 = from_pair(value_own, 1)
-    value_2 = from_pair(value_own, 2)
-    value_3 = from_pair(value_2, 1)
-
-    def routed(k, value_rows):
+    value_u = from_pair(value_own, 1)
+    value_t = from_pair(value_own, top)
+    value_tu = from_pair(value_t, 1)
+
+    def reduced(value_rows):
         part = lax.dot_general(
             value_rows, weights, (((1,), (1,)), ((), ())), preferred_element_type=jnp.float32
         ).astype(jnp.bfloat16)
-        rows = head_sum(part.reshape(n_head, block_rows, width))
+        return head_sum(part.reshape(n_head, block_rows, width))
+
+    def routed(k, rows):
         start = head_rank * block_rows
         places = slot_matrix(
             lax.dynamic_slice_in_dim(owners[k], start, block_rows), capacity, devices_all
@@ -214,18 +222,25 @@
             concat_axis=0,
             tiled=True,
         )
-        return got.reshape(n_hi, QUADS, n_head * capacity, rows.shape[1])
-
-    got = [routed(k, v) for k, v in enumerate((value_own, value_1, value_2, value_3))]
+        return got.reshape(2, n_mid, 2, n_head * capacity, rows.shape[1])
+
+    rows_own = reduced(value_own)
+    value_u, _ = lax.optimization_barrier((value_u, rows_own))
+    got = [routed(0, rows_own)]
+    for k, value_rows in enumerate((value_u, value_t, value_tu)):
+        got.append(routed(k + 1, reduced(value_rows)))
     marks = got[0][..., width:width + 3].astype(jnp.float32)
     keys = jnp.where(marks[..., 2] > 0, marks[..., 0] * 64.0 + marks[..., 1], -1.0)
     whole = keys.reshape(-1, 1)
     equal = jnp.stack([
         (
-            (whole == jnp.concatenate([keys[:, q ^ k].reshape(-1) for k in range(QUADS)]))
+            (whole == jnp.concatenate(
+                [keys[t ^ a, :, u ^ b].reshape(-1) for a in range(2) for b in range(2)]
+            ))
             & (whole >= 0)
         ).astype(jnp.bfloat16)
-        for q in range(QUADS)
+        for t in range(2)
+        for u in range(2)
     ])
     row_grads = merged(equal, got, width)
     return row_grads.reshape(1, devices_all, capacity, QUADS * width)

time: 264 us -> 254 us (0.962)
  waiting for transfers between devices: 152 us -> 143 us
  starting transfers between devices: 46.3 us -> 43.6 us
    all_to_all x1, waiting for transfers between devices: 43.5 us -> 6.68 us  [later_states(): got = lax.all_to_all(sent, 'seq', split_axis=0, concat_axis=0, tiled=True)]
    ppermute x7, waiting for transfers between devices: 46.6 us -> 76.9 us  [from_pair(): return lax.ppermute(array, 'seq', [(i, i ^ k) for i in range(n_seq)])]
  transfers between devices with their start and end apart: 21 -> 21, of which waited for: 12 -> 11; matrix products, arithmetic and copies ran while one was open for 16% -> 19% of each run, Pallas kernels for 0% -> 0%
where the time goes in v4:
time: 254 us; the launch traced here: 253 us
  waiting for transfers between devices  143 us (56%)
  starting transfers between devices  43.6 us (17%)
  matrix products  27.4 us (11%)
  other arithmetic  20.5 us (8%)
  local copies, waits for them, and re-layouts  10.2 us (4%)
  Pallas kernels  7.32 us (3%)
    ppermute x7, waiting for transfers between devices, from_pair(): return lax.ppermute(array, 'seq', [(i, i ^ k) for i in range(n_seq)])  76.9 us
    all_to_all x1, waiting for transfers between devices, later_states(): back = lax.all_to_all(back, 'seq', split_axis=0, concat_axis=0, tiled=True)  22.2 us
    all_to_all x4, waiting for transfers between devices, routed(): lax.all_to_all(sent.reshape(devices_all, capacity, rows.shape[1]), ('seq'...  20.1 us
    ppermute x8, waiting for transfers between devices, head_sum(): got = lax.ppermute(sent, 'head', [(i, i ^ step) for i in range(n_head)])  17.3 us
    all_to_all x4, starting transfers between devices, routed(): lax.all_to_all(sent.reshape(devices_all, capacity, rows.shape[1]), ('seq'...  15.6 us
    dot_general x4, matrix products, reduced(): lax.dot_general(value_rows, weights, (((1,), (1,)), ((), ())), preferred_...  14 us
    ppermute x7, starting transfers between devices, from_pair(): return lax.ppermute(array, 'seq', [(i, i ^ k) for i in range(n_seq)])  10.2 us
    pallas_call x1, Pallas kernels, merged(): pl.pallas_call(merge_kernel, grid=(2, n_mid, 2), in_specs=[pl.BlockSpec((...  7.32 us
  transfers between devices with their start and end apart: 21, of which 11 were waited for; matrix products, arithmetic and copies ran while one was open for 19% of the time, Pallas kernels for 0%

profile of v4, /device:TPU:0, one launch (start us, length us, event | category | flops | bytes accessed | tf_op | source)
XLA Modules:
  0.0 252.7 jit_solution(5882927432023322315)
XLA Ops:
  4.1 1.5 copy.31
  5.7 1.3 broadcast_compare_fusion
  7.1 1.3 fusion.15
  8.3 7.3 %all-to-all-start = ((f32[8,128,128]{2,1,0:T(8,128)}), f32[8,128,128]{2,1,0:T(8,128)S(1)}, u32[]{:S(2)}, u32[]{:S(2)}) async-start(f32[8,128,128]{2,1,0:T(8,128)} %fusion.15), calls=%async_computation | async-start | bytes 1048576 | tf_op jit(solution)/shard_map/all_to_all | solution.py:61
  15.6 2.0 collective-permute-start
  17.6 2.4 collective-permute-start.7
  21.3 1.0 fusion.22
  22.3 1.2 fusion.14
  23.5 6.7 %all-to-all-done = f32[8,128,128]{2,1,0:T(8,128)S(1)} async-done(((f32[8,128,128]{2,1,0:T(8,128)}), f32[8,128,128]{2,1,0:T(8,128)S(1)}, u32[]{:S(2)}, u32[]{:S(2)}) %all-to-all-start) | async-done | bytes 524320 | tf_op jit(solution)/shard_map/all_to_all | solution.py:61
  35.5 3.7 %all-to-all-start.1 = ((bf16[8,128,128]{2,1,0:T(8,128)(2,1)}), bf16[8,128,128]{2,1,0:T(8,128)(2,1)S(1)}, u32[]{:S(2)}, u32[]{:S(2)}) async-start(bf16[8,128,128]{2,1,0:T(8,128)(2,1)} %constant_dynamic-update-slice_fusion), calls=%async_computation.1 | async-start | bytes 524288 | tf_op jit(solution)/shard_map/all_to_all | solution.py:76
  39.2 5.4 %fusion = f32[8,512,128]{1,2,0:T(8,128)S(1)} fusion(f32[512,512]{1,0:T(8,128)} %fusion.14, f32[8]{0:T(128)S(1)} %get-tuple-element.41, pred[512,512]{1,0:T(8,128)(4,1)} %fusion.22, bf16[512,8,128]{0,2,1:T(8,128)(2,1)} %bitcast.134, bf16[512,1024]{1,0:T(8,128)(2,1)} %param.10, bf16[512,1024]{1,0:T(8,128)(2,1)S(1)} %copy-done), kind=kOutput, calls=%fused_computation.1 | convolution fusion | flops 1084227584 | bytes 6553632 | tf_op jit(solution)/shard_map/hst,thf->shf/dot_general | solution.py:24
  44.6 22.2 %all-to-all-done.1 = bf16[8,128,128]{2,1,0:T(8,128)(2,1)S(1)} async-done(((bf16[8,128,128]{2,1,0:T(8,128)(2,1)}), bf16[8,128,128]{2,1,0:T(8,128)(2,1)S(1)}, u32[]{:S(2)}, u32[]{:S(2)}) %all-to-all-start.1) | async-done | bytes 262176 | tf_op jit(solution)/shard_map/all_to_all | solution.py:76
  66.8 1.6 fusion.9
  68.4 2.1 broadcast_select_fusion.1
  70.5 3.9 %convolution_convert_fusion.3 = bf16[512,1536]{1,0:T(8,128)(2,1)S(1)} fusion(bf16[512,1024]{0,1:T(8,128)(2,1)} %bitcast.15, bf16[768,1024]{1,0:T(8,128)(2,1)S(1)} %get-tuple-element.20, bf16[768,1024]{1,0:T(8,128)(2,1)S(1)} %get-tuple-element.19), kind=kOutput, calls=%fused_computation.8 | convolution fusion | flops 1617690624 | bytes 5767168 | tf_op jit(solution)/shard_map/dot_general | solution.py:202
  74.4 0.9 dynamic-slice_bitcast_fusion.3
  76.4 1.4 collective-permute-done.1
  78.1 1.6 collective-permute-start.2
  79.6 44.5 %collective-permute-done.8 = bf16[512,1024]{0,1:T(8,128)(2,1)} collective-permute-done((bf16[512,1024]{0,1:T(8,128)(2,1)}, bf16[512,1024]{0,1:T(8,128)(2,1)}, u32[]{:S(2)}, u32[]{:S(2)}) %collective-permute-start.8) | collective-permute-done | bytes 1048608 | tf_op jit(solution)/shard_map/ppermute | solution.py:161
  124.1 3.1 %convolution_convert_fusion.1 = bf16[512,1536]{1,0:T(8,128)(2,1)S(1)} fusion(bf16[512,1024]{0,1:T(8,128)(2,1)} %collective-permute-done.8, bf16[768,1024]{1,0:T(8,128)(2,1)S(1)} %copy-done.12, bf16[768,1024]{1,0:T(8,128)(2,1)S(1)} %copy-done.9), kind=kOutput, calls=%fused_computation.6 | convolution fusion | flops 1617690624 | bytes 5767168 | tf_op jit(solution)/shard_map/dot_general | solution.py:202
  128.2 1.3 fusion.4
  129.5 2.9 %all-to-all-start.2 = ((bf16[32,8,1664]{2,1,0:T(8,128)(2,1)}), bf16[32,8,1664]{2,1,0:T(8,128)(2,1)S(1)}, u32[]{:S(2)}, u32[]{:S(2)}) async-start(bf16[32,8,1664]{2,1,0:T(8,128)(2,1)} %fusion.4), calls=%async_computation.2 | async-start | bytes 1703936 | tf_op jit(solution)/shard_map/all_to_all | solution.py:218
  132.6 1.6 collective-permute-start.12
  134.2 1.3 fusion.11
  135.5 1.5 collective-permute-start.10
  137.1 3.1 %convolution_convert_fusion.2 = bf16[512,1536]{1,0:T(8,128)(2,1)S(1)} fusion(bf16[512,1024]{0,1:T(8,128)(2,1)} %collective-permute-done.4, bf16[768,1024]{1,0:T(8,128)(2,1)S(1)} %copy-done.13, bf16[768,1024]{1,0:T(8,128)(2,1)S(1)} %copy-done.10), kind=kOutput, calls=%fused_computation.7 | convolution fusion | flops 1617690624 | bytes 5767168 | tf_op jit(solution)/shard_map/dot_general | solution.py:202
  140.3 11.3 %collective-permute-done.10 = bf16[1,128,1536]{2,1,0:T(8,128)(2,1)S(1)} collective-permute-done((bf16[1,128,1536]{2,1,0:T(8,128)(2,1)S(1)}, bf16[1,128,1536]{2,1,0:T(8,128)(2,1)S(1)}, u32[]{:S(2)}, u32[]{:S(2)}) %collective-permute-start.10) | collective-permute-done | bytes 393248 | tf_op jit(solution)/shard_map/ppermute | solution.py:98
  151.6 1.3 fusion.6
  152.9 1.4 all-to-all-done.2
  154.3 4.2 %all-to-all-start.4 = ((bf16[32,8,1536]{2,1,0:T(8,128)(2,1)}), bf16[32,8,1536]{2,1,0:T(8,128)(2,1)S(1)}, u32[]{:S(2)}, u32[]{:S(2)}) async-start(bf16[32,8,1536]{2,1,0:T(8,128)(2,1)} %fusion.6), calls=%async_computation.4 | async-start | bytes 1572864 | tf_op jit(solution)/shard_map/all_to_all | solution.py:218
  158.6 14.2 %collective-permute-done.12 = bf16[512,1024]{0,1:T(8,128)(2,1)} collective-permute-done((bf16[512,1024]{0,1:T(8,128)(2,1)}, bf16[512,1024]{0,1:T(8,128)(2,1)}, u32[]{:S(2)}, u32[]{:S(2)}) %collective-permute-start.12) | collective-permute-done | bytes 1048608 | tf_op jit(solution)/shard_map/ppermute | solution.py:161
  172.8 4.0 %convolution_convert_fusion = bf16[512,1536]{1,0:T(8,128)(2,1)S(1)} fusion(bf16[512,1024]{0,1:T(8,128)(2,1)} %collective-permute-done.12, bf16[768,1024]{1,0:T(8,128)(2,1)} %copy-done.11, bf16[768,1024]{1,0:T(8,128)(2,1)} %copy-done.8), kind=kOutput, calls=%fused_computation.5 | convolution fusion | flops 1617690624 | bytes 5767168 | tf_op jit(solution)/shard_map/dot_general | solution.py:202
  176.9 1.0 dynamic-slice_bitcast_fusion
  177.9 1.3 copy-done.7
  179.1 1.3 fusion.12
  180.5 1.7 collective-permute-start.6
  182.5 3.3 %collective-permute-done.3 = s32[512]{0:T(512)S(1)} collective-permute-done((s32[512]{0:T(512)S(1)}, s32[512]{0:T(512)S(1)}, u32[]{:S(2)}, u32[]{:S(2)}) %collective-permute-start.3) | collective-permute-done | bytes 2080 | tf_op jit(solution)/shard_map/ppermute | solution.py:161
  186.2 4.7 %collective-permute-done.6 = bf16[1,128,1536]{2,1,0:T(8,128)(2,1)S(1)} collective-permute-done((bf16[1,128,1536]{2,1,0:T(8,128)(2,1)S(1)}, bf16[1,128,1536]{2,1,0:T(8,128)(2,1)S(1)}, u32[]{:S(2)}, u32[]{:S(2)}) %collective-permute-start.6) | collective-permute-done | bytes 393248 | tf_op jit(solution)/shard_map/ppermute | solution.py:98
  190.8 1.3 fusion.5
  192.1 5.8 %all-to-all-start.3 = ((bf16[32,8,1536]{2,1,0:T(8,128)(2,1)}), bf16[32,8,1536]{2,1,0:T(8,128)(2,1)S(1)}, u32[]{:S(2)}, u32[]{:S(2)}) async-start(bf16[32,8,1536]{2,1,0:T(8,128)(2,1)} %fusion.5), calls=%async_computation.3 | async-start | bytes 1572864 | tf_op jit(solution)/shard_map/all_to_all | solution.py:218
  197.9 1.6 fusion.10
  199.5 1.8 collective-permute-start.14
  201.4 3.3 %collective-permute-start.11 = (s32[512]{0:T(512)S(1)}, s32[512]{0:T(512)S(1)}, u32[]{:S(2)}, u32[]{:S(2)}) collective-permute-start(s32[512]{0:T(512)S(1)} %bitcast.139), channel_id=1, source_target_pairs={{0,20},{4,16},{8,28},{12,24},{16,4},{20,0},{24,12},{28,8},{1,21},{... | collective-permute-start | bytes 6152 | tf_op jit(solution)/shard_map/ppermute | solution.py:161
  204.7 14.9 %collective-permute-done.11 = s32[512]{0:T(512)S(1)} collective-permute-done((s32[512]{0:T(512)S(1)}, s32[512]{0:T(512)S(1)}, u32[]{:S(2)}, u32[]{:S(2)}) %collective-permute-start.11) | collective-permute-done | bytes 2080 | tf_op jit(solution)/shard_map/ppermute | solution.py:161
  219.9 1.3 fusion.7
  221.2 2.7 %all-to-all-start.5 = ((bf16[32,8,1536]{2,1,0:T(8,128)(2,1)}), bf16[32,8,1536]{2,1,0:T(8,128)(2,1)S(1)}, u32[]{:S(2)}, u32[]{:S(2)}) async-start(bf16[32,8,1536]{2,1,0:T(8,128)(2,1)} %fusion.7), calls=%async_computation.5 | async-start | bytes 1572864 | tf_op jit(solution)/shard_map/all_to_all | solution.py:218
  225.8 18.7 %all-to-all-done.5 = bf16[32,8,1536]{2,1,0:T(8,128)(2,1)S(1)} async-done(((bf16[32,8,1536]{2,1,0:T(8,128)(2,1)}), bf16[32,8,1536]{2,1,0:T(8,128)(2,1)S(1)}, u32[]{:S(2)}, u32[]{:S(2)}) %all-to-all-start.5) | async-done | bytes 786464 | tf_op jit(solution)/shard_map/all_to_all | solution.py:218
  245.3 7.3 %shard_map.82 = bf16[256,6144]{1,0:T(8,128)(2,1)} custom-call(bf16[4,256,256]{2,1,0:T(8,128)(2,1)} %add_convert_fusion.equal, bf16[2,2,2,32,1664]{4,3,2,1,0:T(8,128)(2,1)} %bitcast.121, bf16[2,2,2,32,1536]{4,3,2,1,0:T(8,128)(2,1)} %bitcast.123, bf16[2,2,2,32,1536]{4,3,2,1,0:T(8,128)(2,1)} %bitcast.122, bf16[2,2,2,32,1536]{4,3,2,1,0:T(8,128)(2,1)} %bitcast.124), custom_call_target="tpu_custom_call" | custom-call | tf_op jit(solution)/shard_map/pallas_call | solution.py:117
  (111 shorter events, 17.3 us)
Async XLA Ops:
  0.0 39.1 %copy-start = (bf16[512,1024]{1,0:T(8,128)(2,1)S(1)}, bf16[512,1024]{1,0:T(8,128)(2,1)}, u32[]{:S(2)}) copy-start(bf16[512,1024]{1,0:T(8,128)(2,1)} %param.9) | copy-start | bytes 3145732
  0.0 7.0 %copy-start.16 = (bf16[512,1024]{1,0:T(8,128)(2,1)S(1)}, bf16[512,1024]{1,0:T(8,128)(2,1)}, u32[]{:S(2)}) copy-start(bf16[512,1024]{1,0:T(8,128)(2,1)} %param.10) | copy-start | bytes 3145732
  5.6 2.7 %copy-start.14 = (bf16[512,1024]{0,1:T(8,128)(2,1)}, bf16[512,1024]{0,1:T(8,128)(2,1)S(1)}, u32[]{:S(2)}) copy-start(bf16[512,1024]{0,1:T(8,128)(2,1)S(1)} %copy.31) | copy-start | bytes 3145732
  5.6 12.0 %copy-start.15 = (s32[512,1]{0,1:T(1,128)S(1)}, s32[512,1]{0,1:T(1,128)}, u32[]{:S(2)}) copy-start(s32[512,1]{0,1:T(1,128)} %param.14) | copy-start | bytes 6148
  8.3 21.8 %all-to-all-start = ((f32[8,128,128]{2,1,0:T(8,128)}), f32[8,128,128]{2,1,0:T(8,128)S(1)}, u32[]{:S(2)}, u32[]{:S(2)}) async-start(f32[8,128,128]{2,1,0:T(8,128)} %fusion.15), calls=%async_computation | async-start | bytes 1048576 | tf_op jit(solution)/shard_map/all_to_all | solution.py:61
  15.6 52.7 %collective-permute-start = (bf16[768,1024]{1,0:T(8,128)(2,1)}, bf16[768,1024]{1,0:T(8,128)(2,1)}, u32[]{:S(2)}, u32[]{:S(2)}) collective-permute-start(bf16[768,1024]{1,0:T(8,128)(2,1)} %param.11), channel_id=1, source_target_pairs={{0,8},{4,12},{8,0},{12,4},{16,24},{20,28},{24,16},{28,20},{1,9},{5... | collective-permute-start | bytes 4718600 | tf_op jit(solution)/shard_map/ppermute | solution.py:161
  17.6 58.1 %collective-permute-start.7 = (s32[512]{0:T(512)S(1)}, s32[512]{0:T(512)S(1)}, u32[]{:S(2)}, u32[]{:S(2)}) collective-permute-start(s32[512]{0:T(512)S(1)} %bitcast.137), channel_id=1, source_target_pairs={{0,16},{4,20},{8,24},{12,28},{16,0},{20,4},{24,8},{28,12},{1,17},{... | collective-permute-start | bytes 6152 | tf_op jit(solution)/shard_map/ppermute | solution.py:161
  35.5 31.3 %all-to-all-start.1 = ((bf16[8,128,128]{2,1,0:T(8,128)(2,1)}), bf16[8,128,128]{2,1,0:T(8,128)(2,1)S(1)}, u32[]{:S(2)}, u32[]{:S(2)}) async-start(bf16[8,128,128]{2,1,0:T(8,128)(2,1)} %constant_dynamic-update-slice_fusion), calls=%async_computation.1 | async-start | bytes 524288 | tf_op jit(solution)/shard_map/all_to_all | solution.py:76
  70.4 3.9 %copy-start.8 = (bf16[768,1024]{1,0:T(8,128)(2,1)}, bf16[768,1024]{1,0:T(8,128)(2,1)S(1)}, u32[]{:S(2)}) copy-start(bf16[768,1024]{1,0:T(8,128)(2,1)S(1)} %get-tuple-element.19) | copy-start | bytes 4718596
  70.5 3.9 %copy-start.11 = (bf16[768,1024]{1,0:T(8,128)(2,1)}, bf16[768,1024]{1,0:T(8,128)(2,1)S(1)}, u32[]{:S(2)}) copy-start(bf16[768,1024]{1,0:T(8,128)(2,1)S(1)} %get-tuple-element.20) | copy-start | bytes 4718596
  75.3 2.5 collective-permute-start.1
  75.4 48.7 %collective-permute-start.8 = (bf16[512,1024]{0,1:T(8,128)(2,1)}, bf16[512,1024]{0,1:T(8,128)(2,1)}, u32[]{:S(2)}, u32[]{:S(2)}) collective-permute-start(bf16[512,1024]{0,1:T(8,128)(2,1)} %bitcast.15), channel_id=1, source_target_pairs={{0,16},{4,20},{8,24},{12,28},{16,0},{20,4},{24,8},{28,12},{1,17},{... | collective-permute-start | bytes 3145736 | tf_op jit(solution)/shard_map/ppermute | solution.py:161
  75.8 48.3 %copy-start.9 = (bf16[768,1024]{1,0:T(8,128)(2,1)S(1)}, bf16[768,1024]{1,0:T(8,128)(2,1)}, u32[]{:S(2)}) copy-start(bf16[768,1024]{1,0:T(8,128)(2,1)} %copy-done.8) | copy-start | bytes 4718596
  75.8 48.3 %copy-start.12 = (bf16[768,1024]{1,0:T(8,128)(2,1)S(1)}, bf16[768,1024]{1,0:T(8,128)(2,1)}, u32[]{:S(2)}) copy-start(bf16[768,1024]{1,0:T(8,128)(2,1)} %copy-done.11) | copy-start | bytes 4718596
  76.1 58.1 %collective-permute-start.4 = (bf16[512,1024]{0,1:T(8,128)(2,1)}, bf16[512,1024]{0,1:T(8,128)(2,1)}, u32[]{:S(2)}, u32[]{:S(2)}) collective-permute-start(bf16[512,1024]{0,1:T(8,128)(2,1)} %bitcast.15), channel_id=1, source_target_pairs={{0,4},{4,0},{8,12},{12,8},{16,20},{20,16},{24,28},{28,24},{1,5},{5... | collective-permute-start | bytes 3145736 | tf_op jit(solution)/shard_map/ppermute | solution.py:161
  78.1 50.1 %collective-permute-start.2 = (bf16[1,128,1536]{2,1,0:T(8,128)(2,1)S(1)}, bf16[1,128,1536]{2,1,0:T(8,128)(2,1)S(1)}, u32[]{:S(2)}, u32[]{:S(2)}) collective-permute-start(bf16[1,128,1536]{2,1,0:T(8,128)(2,1)S(1)} %constant_dynamic-slice_fusion.3), channel_id=1, source_target_pairs={{0,2},{1,3},{2,0},{3,1},{4,6},{5,7},{6,4},{7,5},{8,10},{9,11},{10,... | collective-permute-start | bytes 1179656 | tf_op jit(solution)/shard_map/ppermute | solution.py:98
  128.1 6.1 %collective-permute-start.9 = (bf16[2,128,1536]{2,1,0:T(8,128)(2,1)}, bf16[2,128,1536]{2,1,0:T(8,128)(2,1)}, u32[]{:S(2)}, u32[]{:S(2)}) collective-permute-start(bf16[2,128,1536]{2,1,0:T(8,128)(2,1)} %dynamic-slice_bitcast_fusion.1), channel_id=1, source_target_pairs={{0,1},{1,0},{2,3},{3,2},{4,5},{5,4},{6,7},{7,6},{8,9},{9,8},{10,11... | collective-permute-start | bytes 2359304 | tf_op jit(solution)/shard_map/ppermute | solution.py:98
  129.5 24.8 %all-to-all-start.2 = ((bf16[32,8,1664]{2,1,0:T(8,128)(2,1)}), bf16[32,8,1664]{2,1,0:T(8,128)(2,1)S(1)}, u32[]{:S(2)}, u32[]{:S(2)}) async-start(bf16[32,8,1664]{2,1,0:T(8,128)(2,1)} %fusion.4), calls=%async_computation.2 | async-start | bytes 1703936 | tf_op jit(solution)/shard_map/all_to_all | solution.py:218
  132.5 4.6 %copy-start.10 = (bf16[768,1024]{1,0:T(8,128)(2,1)S(1)}, bf16[768,1024]{1,0:T(8,128)(2,1)}, u32[]{:S(2)}) copy-start(bf16[768,1024]{1,0:T(8,128)(2,1)} %copy-done.8) | copy-start | bytes 4718596
  132.5 4.6 %copy-start.13 = (bf16[768,1024]{1,0:T(8,128)(2,1)S(1)}, bf16[768,1024]{1,0:T(8,128)(2,1)}, u32[]{:S(2)}) copy-start(bf16[768,1024]{1,0:T(8,128)(2,1)} %copy-done.11) | copy-start | bytes 4718596
  132.6 40.2 %collective-permute-start.12 = (bf16[512,1024]{0,1:T(8,128)(2,1)}, bf16[512,1024]{0,1:T(8,128)(2,1)}, u32[]{:S(2)}, u32[]{:S(2)}) collective-permute-start(bf16[512,1024]{0,1:T(8,128)(2,1)} %collective-permute-done.8), channel_id=1, source_target_pairs={{0,4},{4,0},{8,12},{12,8},{16,20},{20,16},{24,28},{28,24},{1,5},{5... | collective-permute-start | bytes 3145736 | tf_op jit(solution)/shard_map/ppermute | solution.py:161
  135.5 16.1 %collective-permute-start.10 = (bf16[1,128,1536]{2,1,0:T(8,128)(2,1)S(1)}, bf16[1,128,1536]{2,1,0:T(8,128)(2,1)S(1)}, u32[]{:S(2)}, u32[]{:S(2)}) collective-permute-start(bf16[1,128,1536]{2,1,0:T(8,128)(2,1)S(1)} %constant_dynamic-slice_fusion.1), channel_id=1, source_target_pairs={{0,2},{1,3},{2,0},{3,1},{4,6},{5,7},{6,4},{7,5},{8,10},{9,11},{10,... | collective-permute-start | bytes 1179656 | tf_op jit(solution)/shard_map/ppermute | solution.py:98
  140.1 11.4 %copy-start.6 = (bf16[512,1536]{1,0:T(8,128)(2,1)}, bf16[512,1536]{1,0:T(8,128)(2,1)S(1)}, u32[]{:S(2)}) copy-start(bf16[512,1536]{1,0:T(8,128)(2,1)S(1)} %convolution_convert_fusion.2) | copy-start | bytes 4718596
  140.2 37.6 %collective-permute-start.5 = (bf16[2,128,1536]{2,1,0:T(8,128)(2,1)S(1)}, bf16[2,128,1536]{2,1,0:T(8,128)(2,1)}, u32[]{:S(2)}, u32[]{:S(2)}) collective-permute-start(bf16[2,128,1536]{2,1,0:T(8,128)(2,1)S(1)} %dynamic-slice_bitcast_fusion.2), channel_id=1, source_target_pairs={{0,1},{1,0},{2,3},{3,2},{4,5},{5,4},{6,7},{7,6},{8,9},{9,8},{10,11... | collective-permute-start | bytes 2359304 | tf_op jit(solution)/shard_map/ppermute | solution.py:98
  154.3 69.5 %copy-start.1 = (bf16[32,8,1664]{2,1,0:T(8,128)(2,1)}, bf16[32,8,1664]{2,1,0:T(8,128)(2,1)S(1)}, u32[]{:S(2)}) copy-start(bf16[32,8,1664]{2,1,0:T(8,128)(2,1)S(1)} %all-to-all-done.2) | copy-start | bytes 2555908
  154.3 37.8 %all-to-all-start.4 = ((bf16[32,8,1536]{2,1,0:T(8,128)(2,1)}), bf16[32,8,1536]{2,1,0:T(8,128)(2,1)S(1)}, u32[]{:S(2)}, u32[]{:S(2)}) async-start(bf16[32,8,1536]{2,1,0:T(8,128)(2,1)} %fusion.6), calls=%async_computation.4 | async-start | bytes 1572864 | tf_op jit(solution)/shard_map/all_to_all | solution.py:218
  176.8 3.6 %copy-start.5 = (bf16[512,1536]{1,0:T(8,128)(2,1)}, bf16[512,1536]{1,0:T(8,128)(2,1)S(1)}, u32[]{:S(2)}) copy-start(bf16[512,1536]{1,0:T(8,128)(2,1)S(1)} %convolution_convert_fusion) | copy-start | bytes 4718596
  176.9 2.3 copy-start.7
  177.9 20.0 %collective-permute-start.13 = (bf16[2,128,1536]{2,1,0:T(8,128)(2,1)}, bf16[2,128,1536]{2,1,0:T(8,128)(2,1)}, u32[]{:S(2)}, u32[]{:S(2)}) collective-permute-start(bf16[2,128,1536]{2,1,0:T(8,128)(2,1)} %dynamic-slice_bitcast_fusion), channel_id=1, source_target_pairs={{0,1},{1,0},{2,3},{3,2},{4,5},{5,4},{6,7},{7,6},{8,9},{9,8},{10,11... | collective-permute-start | bytes 2359304 | tf_op jit(solution)/shard_map/ppermute | solution.py:98
  180.5 10.3 %collective-permute-start.6 = (bf16[1,128,1536]{2,1,0:T(8,128)(2,1)S(1)}, bf16[1,128,1536]{2,1,0:T(8,128)(2,1)S(1)}, u32[]{:S(2)}, u32[]{:S(2)}) collective-permute-start(bf16[1,128,1536]{2,1,0:T(8,128)(2,1)S(1)} %constant_dynamic-slice_fusion.2), channel_id=1, source_target_pairs={{0,2},{1,3},{2,0},{3,1},{4,6},{5,7},{6,4},{7,5},{8,10},{9,11},{10,... | collective-permute-start | bytes 1179656 | tf_op jit(solution)/shard_map/ppermute | solution.py:98
  182.2 3.6 %collective-permute-start.3 = (s32[512]{0:T(512)S(1)}, s32[512]{0:T(512)S(1)}, u32[]{:S(2)}, u32[]{:S(2)}) collective-permute-start(s32[512]{0:T(512)S(1)} %bitcast.138), channel_id=1, source_target_pairs={{0,4},{4,0},{8,12},{12,8},{16,20},{20,16},{24,28},{28,24},{1,5},{5... | collective-permute-start | bytes 6152 | tf_op jit(solution)/shard_map/ppermute | solution.py:161
  192.1 7.4 %copy-start.2 = (bf16[32,8,1536]{2,1,0:T(8,128)(2,1)}, bf16[32,8,1536]{2,1,0:T(8,128)(2,1)S(1)}, u32[]{:S(2)}) copy-start(bf16[32,8,1536]{2,1,0:T(8,128)(2,1)S(1)} %all-to-all-done.4) | copy-start | bytes 2359300
  192.1 29.0 %all-to-all-start.3 = ((bf16[32,8,1536]{2,1,0:T(8,128)(2,1)}), bf16[32,8,1536]{2,1,0:T(8,128)(2,1)S(1)}, u32[]{:S(2)}, u32[]{:S(2)}) async-start(bf16[32,8,1536]{2,1,0:T(8,128)(2,1)} %fusion.5), calls=%async_computation.3 | async-start | bytes 1572864 | tf_op jit(solution)/shard_map/all_to_all | solution.py:218
  199.5 20.4 %collective-permute-start.14 = (bf16[1,128,1536]{2,1,0:T(8,128)(2,1)S(1)}, bf16[1,128,1536]{2,1,0:T(8,128)(2,1)S(1)}, u32[]{:S(2)}, u32[]{:S(2)}) collective-permute-start(bf16[1,128,1536]{2,1,0:T(8,128)(2,1)S(1)} %constant_dynamic-slice_fusion), channel_id=1, source_target_pairs={{0,2},{1,3},{2,0},{3,1},{4,6},{5,7},{6,4},{7,5},{8,10},{9,11},{10,... | collective-permute-start | bytes 1179656 | tf_op jit(solution)/shard_map/ppermute | solution.py:98
  201.4 18.2 %collective-permute-start.11 = (s32[512]{0:T(512)S(1)}, s32[512]{0:T(512)S(1)}, u32[]{:S(2)}, u32[]{:S(2)}) collective-permute-start(s32[512]{0:T(512)S(1)} %bitcast.139), channel_id=1, source_target_pairs={{0,20},{4,16},{8,28},{12,24},{16,4},{20,0},{24,12},{28,8},{1,21},{... | collective-permute-start | bytes 6152 | tf_op jit(solution)/shard_map/ppermute | solution.py:161
  221.2 23.3 %copy-start.3 = (bf16[32,8,1536]{2,1,0:T(8,128)(2,1)}, bf16[32,8,1536]{2,1,0:T(8,128)(2,1)S(1)}, u32[]{:S(2)}) copy-start(bf16[32,8,1536]{2,1,0:T(8,128)(2,1)S(1)} %all-to-all-done.3) | copy-start | bytes 2359300
  221.2 23.3 %all-to-all-start.5 = ((bf16[32,8,1536]{2,1,0:T(8,128)(2,1)}), bf16[32,8,1536]{2,1,0:T(8,128)(2,1)S(1)}, u32[]{:S(2)}, u32[]{:S(2)}) async-start(bf16[32,8,1536]{2,1,0:T(8,128)(2,1)} %fusion.7), calls=%async_computation.5 | async-start | bytes 1572864 | tf_op jit(solution)/shard_map/all_to_all | solution.py:218
  244.5 0.9 copy-start.4

commit v5 on v4

--- a/solution.py
+++ b/solution.py
@@ -196,7 +196,6 @@
     )
     value_u = from_pair(value_own, 1)
     value_t = from_pair(value_own, top)
-    value_tu = from_pair(value_t, 1)
 
     def reduced(value_rows):
         part = lax.dot_general(
@@ -226,9 +225,12 @@
 
     rows_own = reduced(value_own)
     value_u, _ = lax.optimization_barrier((value_u, rows_own))
-    got = [routed(0, rows_own)]
-    for k, value_rows in enumerate((value_u, value_t, value_tu)):
-        got.append(routed(k + 1, reduced(value_rows)))
+    rows_u = reduced(value_u)
+    value_t, _ = lax.optimization_barrier((value_t, rows_u))
+    value_tu = from_pair(value_t, 1)
+    got = [routed(0, rows_own), routed(1, rows_u)]
+    for k, value_rows in enumerate((value_t, value_tu)):
+        got.append(routed(k + 2, reduced(value_rows)))
     marks = got[0][..., width:width + 3].astype(jnp.float32)
     keys = jnp.where(marks[..., 2] > 0, marks[..., 0] * 64.0 + marks[..., 1], -1.0)
     whole = keys.reshape(-1, 1)

time: 254 us -> 283 us (1.11)
  waiting for transfers between devices: 143 us -> 173 us
    ppermute x7, waiting for transfers between devices: 76.9 us -> 100 us  [from_pair(): return lax.ppermute(array, 'seq', [(i, i ^ k) for i in range(n_seq)])]
    ppermute x8, waiting for transfers between devices: 17.3 us -> 21.3 us  [head_sum(): got = lax.ppermute(sent, 'head', [(i, i ^ step) for i in range(n_head)])]
    all_to_all x1, waiting for transfers between devices: 6.68 us -> 10.1 us  [later_states(): got = lax.all_to_all(sent, 'seq', split_axis=0, concat_axis=0, tiled=True)]
  transfers between devices with their start and end apart: 21 -> 21, of which waited for: 11 -> 12; matrix products, arithmetic and copies ran while one was open for 19% -> 14% of each run, Pallas kernels for 0% -> 0%
where the time goes in v5:
time: 283 us; the launch traced here: 282 us
  waiting for transfers between devices  173 us (61%)
  starting transfers between devices  41.9 us (15%)
  matrix products  28.9 us (10%)
  other arithmetic  22.1 us (8%)
  local copies, waits for them, and re-layouts  8.42 us (3%)
  Pallas kernels  7.32 us (3%)
    ppermute x7, waiting for transfers between devices, from_pair(): return lax.ppermute(array, 'seq', [(i, i ^ k) for i in range(n_seq)])  100 us
    all_to_all x1, waiting for transfers between devices, later_states(): back = lax.all_to_all(back, 'seq', split_axis=0, concat_axis=0, tiled=True)  22.1 us
    ppermute x8, waiting for transfers between devices, head_sum(): got = lax.ppermute(sent, 'head', [(i, i ^ step) for i in range(n_head)])  21.3 us
    all_to_all x4, waiting for transfers between devices, routed(): lax.all_to_all(sent.reshape(devices_all, capacity, rows.shape[1]), ('seq'...  18.7 us
    dot_general x4, matrix products, reduced(): lax.dot_general(value_rows, weights, (((1,), (1,)), ((), ())), preferred_...  15.5 us
    all_to_all x4, starting transfers between devices, routed(): lax.all_to_all(sent.reshape(devices_all, capacity, rows.shape[1]), ('seq'...  13.7 us
    ppermute x7, starting transfers between devices, from_pair(): return lax.ppermute(array, 'seq', [(i, i ^ k) for i in range(n_seq)])  10.1 us
    all_to_all x1, waiting for transfers between devices, later_states(): got = lax.all_to_all(sent, 'seq', split_axis=0, concat_axis=0, tiled=True)  10.1 us
  transfers between devices with their start and end apart: 21, of which 12 were waited for; matrix products, arithmetic and copies ran while one was open for 14% of the time, Pallas kernels for 0%

profile of v5, /device:TPU:0, one launch (start us, length us, event | category | flops | bytes accessed | tf_op | source)
XLA Modules:
  0.0 281.6 jit_solution(3921822450335536898)
XLA Ops:
  4.1 1.5 copy.31
  5.6 1.2 broadcast_compare_fusion
  6.9 1.3 fusion.15
  8.2 7.3 %all-to-all-start = ((f32[8,128,128]{2,1,0:T(8,128)}), f32[8,128,128]{2,1,0:T(8,128)S(1)}, u32[]{:S(2)}, u32[]{:S(2)}) async-start(f32[8,128,128]{2,1,0:T(8,128)} %fusion.15), calls=%async_computation | async-start | bytes 1048576 | tf_op jit(solution)/shard_map/all_to_all | solution.py:61
  15.5 2.0 collective-permute-start
  17.8 1.0 fusion.22
  18.8 1.2 fusion.14
  19.9 10.1 %all-to-all-done = f32[8,128,128]{2,1,0:T(8,128)S(1)} async-done(((f32[8,128,128]{2,1,0:T(8,128)}), f32[8,128,128]{2,1,0:T(8,128)S(1)}, u32[]{:S(2)}, u32[]{:S(2)}) %all-to-all-start) | async-done | bytes 524320 | tf_op jit(solution)/shard_map/all_to_all | solution.py:61
  35.3 3.7 %all-to-all-start.1 = ((bf16[8,128,128]{2,1,0:T(8,128)(2,1)}), bf16[8,128,128]{2,1,0:T(8,128)(2,1)S(1)}, u32[]{:S(2)}, u32[]{:S(2)}) async-start(bf16[8,128,128]{2,1,0:T(8,128)(2,1)} %constant_dynamic-update-slice_fusion), calls=%async_computation.1 | async-start | bytes 524288 | tf_op jit(solution)/shard_map/all_to_all | solution.py:76
  39.1 5.4 %fusion = f32[8,512,128]{1,2,0:T(8,128)S(1)} fusion(f32[512,512]{1,0:T(8,128)} %fusion.14, f32[8]{0:T(128)S(1)} %get-tuple-element.43, pred[512,512]{1,0:T(8,128)(4,1)} %fusion.22, bf16[512,8,128]{0,2,1:T(8,128)(2,1)} %bitcast.134, bf16[512,1024]{1,0:T(8,128)(2,1)} %param.10, bf16[512,1024]{1,0:T(8,128)(2,1)S(1)} %copy-done), kind=kOutput, calls=%fused_computation.1 | convolution fusion | flops 1084227584 | bytes 6553632 | tf_op jit(solution)/shard_map/hst,thf->shf/dot_general | solution.py:24
  44.5 22.1 %all-to-all-done.1 = bf16[8,128,128]{2,1,0:T(8,128)(2,1)S(1)} async-done(((bf16[8,128,128]{2,1,0:T(8,128)(2,1)}), bf16[8,128,128]{2,1,0:T(8,128)(2,1)S(1)}, u32[]{:S(2)}, u32[]{:S(2)}) %all-to-all-start.1) | async-done | bytes 262176 | tf_op jit(solution)/shard_map/all_to_all | solution.py:76
  66.6 1.5 fusion.9
  68.1 2.1 broadcast_select_fusion.1
  70.2 3.9 %convolution_convert_fusion.3 = bf16[512,1536]{1,0:T(8,128)(2,1)S(1)} fusion(bf16[512,1024]{0,1:T(8,128)(2,1)} %bitcast.15, bf16[768,1024]{1,0:T(8,128)(2,1)S(1)} %get-tuple-element.22, bf16[768,1024]{1,0:T(8,128)(2,1)S(1)} %get-tuple-element.21), kind=kOutput, calls=%fused_computation.8 | convolution fusion | flops 1617690624 | bytes 5767168 | tf_op jit(solution)/shard_map/dot_general | solution.py:201
  74.4 2.3 collective-permute-done.1
  76.6 1.3 fusion.13
  78.0 1.6 collective-permute-start.2
  79.6 9.7 %collective-permute-done.2 = bf16[1,128,1536]{2,1,0:T(8,128)(2,1)S(1)} collective-permute-done((bf16[1,128,1536]{2,1,0:T(8,128)(2,1)S(1)}, bf16[1,128,1536]{2,1,0:T(8,128)(2,1)S(1)}, u32[]{:S(2)}, u32[]{:S(2)}) %collective-permute-start.2) | collective-permute-done | bytes 393248 | tf_op jit(solution)/shard_map/ppermute | solution.py:98
  89.3 10.8 %collective-permute-done.4 = bf16[512,1024]{0,1:T(8,128)(2,1)} collective-permute-done((bf16[512,1024]{0,1:T(8,128)(2,1)}, bf16[512,1024]{0,1:T(8,128)(2,1)}, u32[]{:S(2)}, u32[]{:S(2)}) %collective-permute-start.4) | collective-permute-done | bytes 1048608 | tf_op jit(solution)/shard_map/ppermute | solution.py:161
  100.1 4.0 %convolution_convert_fusion.2 = bf16[512,1536]{1,0:T(8,128)(2,1)S(1)} fusion(bf16[512,1024]{0,1:T(8,128)(2,1)} %collective-permute-done.4, bf16[768,1024]{1,0:T(8,128)(2,1)} %copy-done.10, bf16[768,1024]{1,0:T(8,128)(2,1)} %copy-done.8), kind=kOutput, calls=%fused_computation.7 | convolution fusion | flops 1617690624 | bytes 5767168 | tf_op jit(solution)/shard_map/dot_general | solution.py:201
  104.2 1.1 copy-done.6
  106.6 1.1 collective-permute-done.5
  107.7 1.3 fusion.12
  109.1 1.6 collective-permute-start.6
  111.0 1.3 fusion.4
  112.3 2.8 all-to-all-start.2
  115.1 8.3 %collective-permute-done.6 = bf16[1,128,1536]{2,1,0:T(8,128)(2,1)S(1)} collective-permute-done((bf16[1,128,1536]{2,1,0:T(8,128)(2,1)S(1)}, bf16[1,128,1536]{2,1,0:T(8,128)(2,1)S(1)}, u32[]{:S(2)}, u32[]{:S(2)}) %collective-permute-start.6) | collective-permute-done | bytes 393248 | tf_op jit(solution)/shard_map/ppermute | solution.py:98
  123.5 40.7 %collective-permute-done.8 = bf16[512,1024]{0,1:T(8,128)(2,1)} collective-permute-done((bf16[512,1024]{0,1:T(8,128)(2,1)}, bf16[512,1024]{0,1:T(8,128)(2,1)}, u32[]{:S(2)}, u32[]{:S(2)}) %collective-permute-start.8) | collective-permute-done | bytes 1048608 | tf_op jit(solution)/shard_map/ppermute | solution.py:161
  164.2 4.0 %convolution_convert_fusion.1 = bf16[512,1536]{1,0:T(8,128)(2,1)S(1)} fusion(bf16[512,1024]{0,1:T(8,128)(2,1)} %collective-permute-done.8, bf16[768,1024]{1,0:T(8,128)(2,1)} %copy-done.10, bf16[768,1024]{1,0:T(8,128)(2,1)} %copy-done.8), kind=kOutput, calls=%fused_computation.6 | convolution fusion | flops 1617690624 | bytes 5767168 | tf_op jit(solution)/shard_map/dot_general | solution.py:201
  168.5 1.3 collective-permute-start.12
  170.5 24.2 %collective-permute-done.3 = s32[512]{0:T(512)S(1)} collective-permute-done((s32[512]{0:T(512)S(1)}, s32[512]{0:T(512)S(1)}, u32[]{:S(2)}, u32[]{:S(2)}) %collective-permute-start.3) | collective-permute-done | bytes 2080 | tf_op jit(solution)/shard_map/ppermute | solution.py:161
  195.1 1.3 fusion.5
  196.3 3.0 %all-to-all-start.3 = ((bf16[32,8,1536]{2,1,0:T(8,128)(2,1)}), bf16[32,8,1536]{2,1,0:T(8,128)(2,1)S(1)}, u32[]{:S(2)}, u32[]{:S(2)}) async-start(bf16[32,8,1536]{2,1,0:T(8,128)(2,1)} %fusion.5), calls=%async_computation.3 | async-start | bytes 1572864 | tf_op jit(solution)/shard_map/all_to_all | solution.py:217
  199.3 1.7 fusion.11
  201.2 3.6 %convolution_convert_fusion = bf16[512,1536]{1,0:T(8,128)(2,1)S(1)} fusion(bf16[512,1024]{0,1:T(8,128)(2,1)} %collective-permute-done.12, bf16[768,1024]{1,0:T(8,128)(2,1)} %copy-done.10, bf16[768,1024]{1,0:T(8,128)(2,1)S(1)} %copy-done.9), kind=kOutput, calls=%fused_computation.5 | convolution fusion | flops 1617690624 | bytes 5767168 | tf_op jit(solution)/shard_map/dot_general | solution.py:201
  206.0 1.7 collective-permute-start.10
  207.8 2.4 collective-permute-start.7
  210.2 9.8 %collective-permute-done.7 = s32[512]{0:T(512)S(1)} collective-permute-done((s32[512]{0:T(512)S(1)}, s32[512]{0:T(512)S(1)}, u32[]{:S(2)}, u32[]{:S(2)}) %collective-permute-start.7) | collective-permute-done | bytes 2080 | tf_op jit(solution)/shard_map/ppermute | solution.py:161
  220.3 1.3 fusion.6
  221.6 5.2 %all-to-all-start.4 = ((bf16[32,8,1536]{2,1,0:T(8,128)(2,1)}), bf16[32,8,1536]{2,1,0:T(8,128)(2,1)S(1)}, u32[]{:S(2)}, u32[]{:S(2)}) async-start(bf16[32,8,1536]{2,1,0:T(8,128)(2,1)} %fusion.6), calls=%async_computation.4 | async-start | bytes 1572864 | tf_op jit(solution)/shard_map/all_to_all | solution.py:217
  226.9 1.6 fusion.10
  228.5 1.8 collective-permute-start.14
  230.3 3.3 %collective-permute-start.11 = (s32[512]{0:T(512)S(1)}, s32[512]{0:T(512)S(1)}, u32[]{:S(2)}, u32[]{:S(2)}) collective-permute-start(s32[512]{0:T(512)S(1)} %bitcast.139), channel_id=1, source_target_pairs={{0,20},{4,16},{8,28},{12,24},{16,4},{20,0},{24,12},{28,8},{1,21},{... | collective-permute-start | bytes 6152 | tf_op jit(solution)/shard_map/ppermute | solution.py:161
  233.6 14.9 %collective-permute-done.11 = s32[512]{0:T(512)S(1)} collective-permute-done((s32[512]{0:T(512)S(1)}, s32[512]{0:T(512)S(1)}, u32[]{:S(2)}, u32[]{:S(2)}) %collective-permute-start.11) | collective-permute-done | bytes 2080 | tf_op jit(solution)/shard_map/ppermute | solution.py:161
  248.9 1.3 fusion.7
  250.1 2.7 all-to-all-start.5
  254.8 18.7 %all-to-all-done.5 = bf16[32,8,1536]{2,1,0:T(8,128)(2,1)S(1)} async-done(((bf16[32,8,1536]{2,1,0:T(8,128)(2,1)}), bf16[32,8,1536]{2,1,0:T(8,128)(2,1)S(1)}, u32[]{:S(2)}, u32[]{:S(2)}) %all-to-all-start.5) | async-done | bytes 786464 | tf_op jit(solution)/shard_map/all_to_all | solution.py:217
  274.3 7.3 %shard_map.82 = bf16[256,6144]{1,0:T(8,128)(2,1)} custom-call(bf16[4,256,256]{2,1,0:T(8,128)(2,1)} %add_convert_fusion.equal, bf16[2,2,2,32,1664]{4,3,2,1,0:T(8,128)(2,1)} %bitcast.121, bf16[2,2,2,32,1536]{4,3,2,1,0:T(8,128)(2,1)} %bitcast.122, bf16[2,2,2,32,1536]{4,3,2,1,0:T(8,128)(2,1)} %bitcast.123, bf16[2,2,2,32,1536]{4,3,2,1,0:T(8,128)(2,1)} %bitcast.124), custom_call_target="tpu_custom_call" | custom-call | tf_op jit(solution)/shard_map/pallas_call | solution.py:117
  (106 shorter events, 18.1 us)
Async XLA Ops:
  0.0 39.0 %copy-start = (bf16[512,1024]{1,0:T(8,128)(2,1)S(1)}, bf16[512,1024]{1,0:T(8,128)(2,1)}, u32[]{:S(2)}) copy-start(bf16[512,1024]{1,0:T(8,128)(2,1)} %param.9) | copy-start | bytes 3145732
  0.0 6.9 %copy-start.13 = (bf16[512,1024]{1,0:T(8,128)(2,1)S(1)}, bf16[512,1024]{1,0:T(8,128)(2,1)}, u32[]{:S(2)}) copy-start(bf16[512,1024]{1,0:T(8,128)(2,1)} %param.10) | copy-start | bytes 3145732
  5.6 2.6 copy-start.11
  8.2 21.8 %all-to-all-start = ((f32[8,128,128]{2,1,0:T(8,128)}), f32[8,128,128]{2,1,0:T(8,128)S(1)}, u32[]{:S(2)}, u32[]{:S(2)}) async-start(f32[8,128,128]{2,1,0:T(8,128)} %fusion.15), calls=%async_computation | async-start | bytes 1048576 | tf_op jit(solution)/shard_map/all_to_all | solution.py:61
  15.5 52.6 %collective-permute-start = (bf16[768,1024]{1,0:T(8,128)(2,1)}, bf16[768,1024]{1,0:T(8,128)(2,1)}, u32[]{:S(2)}, u32[]{:S(2)}) collective-permute-start(bf16[768,1024]{1,0:T(8,128)(2,1)} %param.11), channel_id=1, source_target_pairs={{0,8},{4,12},{8,0},{12,4},{16,24},{20,28},{24,16},{28,20},{1,9},{5... | collective-permute-start | bytes 4718600 | tf_op jit(solution)/shard_map/ppermute | solution.py:161
  35.3 31.3 %all-to-all-start.1 = ((bf16[8,128,128]{2,1,0:T(8,128)(2,1)}), bf16[8,128,128]{2,1,0:T(8,128)(2,1)S(1)}, u32[]{:S(2)}, u32[]{:S(2)}) async-start(bf16[8,128,128]{2,1,0:T(8,128)(2,1)} %constant_dynamic-update-slice_fusion), calls=%async_computation.1 | async-start | bytes 524288 | tf_op jit(solution)/shard_map/all_to_all | solution.py:76
  70.2 3.9 %copy-start.8 = (bf16[768,1024]{1,0:T(8,128)(2,1)}, bf16[768,1024]{1,0:T(8,128)(2,1)S(1)}, u32[]{:S(2)}) copy-start(bf16[768,1024]{1,0:T(8,128)(2,1)S(1)} %get-tuple-element.21) | copy-start | bytes 4718596
  70.2 3.9 %copy-start.10 = (bf16[768,1024]{1,0:T(8,128)(2,1)}, bf16[768,1024]{1,0:T(8,128)(2,1)S(1)}, u32[]{:S(2)}) copy-start(bf16[768,1024]{1,0:T(8,128)(2,1)S(1)} %get-tuple-element.22) | copy-start | bytes 4718596
  74.2 2.5 collective-permute-start.1
  74.3 25.8 %collective-permute-start.4 = (bf16[512,1024]{0,1:T(8,128)(2,1)}, bf16[512,1024]{0,1:T(8,128)(2,1)}, u32[]{:S(2)}, u32[]{:S(2)}) collective-permute-start(bf16[512,1024]{0,1:T(8,128)(2,1)} %bitcast.15), channel_id=1, source_target_pairs={{0,4},{4,0},{8,12},{12,8},{16,20},{20,16},{24,28},{28,24},{1,5},{5... | collective-permute-start | bytes 3145736 | tf_op jit(solution)/shard_map/ppermute | solution.py:161
  78.0 11.2 %collective-permute-start.2 = (bf16[1,128,1536]{2,1,0:T(8,128)(2,1)S(1)}, bf16[1,128,1536]{2,1,0:T(8,128)(2,1)S(1)}, u32[]{:S(2)}, u32[]{:S(2)}) collective-permute-start(bf16[1,128,1536]{2,1,0:T(8,128)(2,1)S(1)} %constant_dynamic-slice_fusion.3), channel_id=1, source_target_pairs={{0,2},{1,3},{2,0},{3,1},{4,6},{5,7},{6,4},{7,5},{8,10},{9,11},{10,... | collective-permute-start | bytes 1179656 | tf_op jit(solution)/shard_map/ppermute | solution.py:98
  89.3 17.0 %copy-start.12 = (s32[512,1]{0,1:T(1,128)S(1)}, s32[512,1]{0,1:T(1,128)}, u32[]{:S(2)}) copy-start(s32[512,1]{0,1:T(1,128)} %param.14) | copy-start | bytes 6148
  104.2 1.2 copy-start.6
  105.4 2.4 collective-permute-start.5
  106.4 57.8 %collective-permute-start.8 = (bf16[512,1024]{0,1:T(8,128)(2,1)}, bf16[512,1024]{0,1:T(8,128)(2,1)}, u32[]{:S(2)}, u32[]{:S(2)}) collective-permute-start(bf16[512,1024]{0,1:T(8,128)(2,1)} %bitcast.15), channel_id=1, source_target_pairs={{0,16},{4,20},{8,24},{12,28},{16,0},{20,4},{24,8},{28,12},{1,17},{... | collective-permute-start | bytes 3145736 | tf_op jit(solution)/shard_map/ppermute | solution.py:161
  109.1 14.3 %collective-permute-start.6 = (bf16[1,128,1536]{2,1,0:T(8,128)(2,1)S(1)}, bf16[1,128,1536]{2,1,0:T(8,128)(2,1)S(1)}, u32[]{:S(2)}, u32[]{:S(2)}) collective-permute-start(bf16[1,128,1536]{2,1,0:T(8,128)(2,1)S(1)} %constant_dynamic-slice_fusion.2), channel_id=1, source_target_pairs={{0,2},{1,3},{2,0},{3,1},{4,6},{5,7},{6,4},{7,5},{8,10},{9,11},{10,... | collective-permute-start | bytes 1179656 | tf_op jit(solution)/shard_map/ppermute | solution.py:98
  112.3 84.0 %all-to-all-start.2 = ((bf16[32,8,1664]{2,1,0:T(8,128)(2,1)}), bf16[32,8,1664]{2,1,0:T(8,128)(2,1)S(1)}, u32[]{:S(2)}, u32[]{:S(2)}) async-start(bf16[32,8,1664]{2,1,0:T(8,128)(2,1)} %fusion.4), calls=%async_computation.2 | async-start | bytes 1703936 | tf_op jit(solution)/shard_map/all_to_all | solution.py:217
  168.3 26.8 %copy-start.7 = (bf16[512,1536]{1,0:T(8,128)(2,1)}, bf16[512,1536]{1,0:T(8,128)(2,1)S(1)}, u32[]{:S(2)}) copy-start(bf16[512,1536]{1,0:T(8,128)(2,1)S(1)} %convolution_convert_fusion.1) | copy-start | bytes 4718596
  168.4 30.9 %collective-permute-start.9 = (bf16[2,128,1536]{2,1,0:T(8,128)(2,1)S(1)}, bf16[2,128,1536]{2,1,0:T(8,128)(2,1)}, u32[]{:S(2)}, u32[]{:S(2)}) collective-permute-start(bf16[2,128,1536]{2,1,0:T(8,128)(2,1)S(1)} %dynamic-slice_bitcast_fusion.1), channel_id=1, source_target_pairs={{0,1},{1,0},{2,3},{3,2},{4,5},{5,4},{6,7},{7,6},{8,9},{9,8},{10,11... | collective-permute-start | bytes 2359304 | tf_op jit(solution)/shard_map/ppermute | solution.py:98
  168.5 32.5 %collective-permute-start.12 = (bf16[512,1024]{0,1:T(8,128)(2,1)}, bf16[512,1024]{0,1:T(8,128)(2,1)}, u32[]{:S(2)}, u32[]{:S(2)}) collective-permute-start(bf16[512,1024]{0,1:T(8,128)(2,1)} %collective-permute-done.8), channel_id=1, source_target_pairs={{0,4},{4,0},{8,12},{12,8},{16,20},{20,16},{24,28},{28,24},{1,5},{5... | collective-permute-start | bytes 3145736 | tf_op jit(solution)/shard_map/ppermute | solution.py:161
  169.7 25.0 %collective-permute-start.3 = (s32[512]{0:T(512)S(1)}, s32[512]{0:T(512)S(1)}, u32[]{:S(2)}, u32[]{:S(2)}) collective-permute-start(s32[512]{0:T(512)S(1)} %bitcast.137), channel_id=1, source_target_pairs={{0,4},{4,0},{8,12},{12,8},{16,20},{20,16},{24,28},{28,24},{1,5},{5... | collective-permute-start | bytes 6152 | tf_op jit(solution)/shard_map/ppermute | solution.py:161
  196.3 56.5 %copy-start.1 = (bf16[32,8,1664]{2,1,0:T(8,128)(2,1)}, bf16[32,8,1664]{2,1,0:T(8,128)(2,1)S(1)}, u32[]{:S(2)}) copy-start(bf16[32,8,1664]{2,1,0:T(8,128)(2,1)S(1)} %all-to-all-done.2) | copy-start | bytes 2555908
  196.3 25.3 %all-to-all-start.3 = ((bf16[32,8,1536]{2,1,0:T(8,128)(2,1)}), bf16[32,8,1536]{2,1,0:T(8,128)(2,1)S(1)}, u32[]{:S(2)}, u32[]{:S(2)}) async-start(bf16[32,8,1536]{2,1,0:T(8,128)(2,1)} %fusion.5), calls=%async_computation.3 | async-start | bytes 1572864 | tf_op jit(solution)/shard_map/all_to_all | solution.py:217
  199.3 1.9 copy-start.9
  204.8 15.6 %copy-start.5 = (bf16[512,1536]{1,0:T(8,128)(2,1)}, bf16[512,1536]{1,0:T(8,128)(2,1)S(1)}, u32[]{:S(2)}) copy-start(bf16[512,1536]{1,0:T(8,128)(2,1)S(1)} %convolution_convert_fusion) | copy-start | bytes 4718596
  205.8 21.1 %collective-permute-start.13 = (bf16[2,128,1536]{2,1,0:T(8,128)(2,1)}, bf16[2,128,1536]{2,1,0:T(8,128)(2,1)}, u32[]{:S(2)}, u32[]{:S(2)}) collective-permute-start(bf16[2,128,1536]{2,1,0:T(8,128)(2,1)} %dynamic-slice_bitcast_fusion), channel_id=1, source_target_pairs={{0,1},{1,0},{2,3},{3,2},{4,5},{5,4},{6,7},{7,6},{8,9},{9,8},{10,11... | collective-permute-start | bytes 2359304 | tf_op jit(solution)/shard_map/ppermute | solution.py:98
  206.0 14.3 %collective-permute-start.10 = (bf16[1,128,1536]{2,1,0:T(8,128)(2,1)S(1)}, bf16[1,128,1536]{2,1,0:T(8,128)(2,1)S(1)}, u32[]{:S(2)}, u32[]{:S(2)}) collective-permute-start(bf16[1,128,1536]{2,1,0:T(8,128)(2,1)S(1)} %constant_dynamic-slice_fusion.1), channel_id=1, source_target_pairs={{0,2},{1,3},{2,0},{3,1},{4,6},{5,7},{6,4},{7,5},{8,10},{9,11},{10,... | collective-permute-start | bytes 1179656 | tf_op jit(solution)/shard_map/ppermute | solution.py:98
  207.8 12.2 %collective-permute-start.7 = (s32[512]{0:T(512)S(1)}, s32[512]{0:T(512)S(1)}, u32[]{:S(2)}, u32[]{:S(2)}) collective-permute-start(s32[512]{0:T(512)S(1)} %bitcast.138), channel_id=1, source_target_pairs={{0,16},{4,20},{8,24},{12,28},{16,0},{20,4},{24,8},{28,12},{1,17},{... | collective-permute-start | bytes 6152 | tf_op jit(solution)/shard_map/ppermute | solution.py:161
  221.6 6.8 %copy-start.2 = (bf16[32,8,1536]{2,1,0:T(8,128)(2,1)}, bf16[32,8,1536]{2,1,0:T(8,128)(2,1)S(1)}, u32[]{:S(2)}) copy-start(bf16[32,8,1536]{2,1,0:T(8,128)(2,1)S(1)} %all-to-all-done.3) | copy-start | bytes 2359300
  221.6 28.5 %all-to-all-start.4 = ((bf16[32,8,1536]{2,1,0:T(8,128)(2,1)}), bf16[32,8,1536]{2,1,0:T(8,128)(2,1)S(1)}, u32[]{:S(2)}, u32[]{:S(2)}) async-start(bf16[32,8,1536]{2,1,0:T(8,128)(2,1)} %fusion.6), calls=%async_computation.4 | async-start | bytes 1572864 | tf_op jit(solution)/shard_map/all_to_all | solution.py:217
  228.5 20.4 %collective-permute-start.14 = (bf16[1,128,1536]{2,1,0:T(8,128)(2,1)S(1)}, bf16[1,128,1536]{2,1,0:T(8,128)(2,1)S(1)}, u32[]{:S(2)}, u32[]{:S(2)}) collective-permute-start(bf16[1,128,1536]{2,1,0:T(8,128)(2,1)S(1)} %constant_dynamic-slice_fusion), channel_id=1, source_target_pairs={{0,2},{1,3},{2,0},{3,1},{4,6},{5,7},{6,4},{7,5},{8,10},{9,11},{10,... | collective-permute-start | bytes 1179656 | tf_op jit(solution)/shard_map/ppermute | solution.py:98
  230.3 18.2 %collective-permute-start.11 = (s32[512]{0:T(512)S(1)}, s32[512]{0:T(512)S(1)}, u32[]{:S(2)}, u32[]{:S(2)}) collective-permute-start(s32[512]{0:T(512)S(1)} %bitcast.139), channel_id=1, source_target_pairs={{0,20},{4,16},{8,28},{12,24},{16,4},{20,0},{24,12},{28,8},{1,21},{... | collective-permute-start | bytes 6152 | tf_op jit(solution)/shard_map/ppermute | solution.py:161
  250.1 23.3 %copy-start.3 = (bf16[32,8,1536]{2,1,0:T(8,128)(2,1)}, bf16[32,8,1536]{2,1,0:T(8,128)(2,1)S(1)}, u32[]{:S(2)}) copy-start(bf16[32,8,1536]{2,1,0:T(8,128)(2,1)S(1)} %all-to-all-done.4) | copy-start | bytes 2359300
  250.1 23.3 %all-to-all-start.5 = ((bf16[32,8,1536]{2,1,0:T(8,128)(2,1)}), bf16[32,8,1536]{2,1,0:T(8,128)(2,1)S(1)}, u32[]{:S(2)}, u32[]{:S(2)}) async-start(bf16[32,8,1536]{2,1,0:T(8,128)(2,1)} %fusion.7), calls=%async_computation.5 | async-start | bytes 1572864 | tf_op jit(solution)/shard_map/all_to_all | solution.py:217
  273.4 0.9 copy-start.4
